TPU v7x, 32 devices: a whole 2x2x4 slice. The times are simulated.
32 devices in a mesh: leaf: 8 (over y, x, core), sib: 4 (over z).
Axes of the slice: x: 2, y: 2, z: 4, core: 2. Of those that a mesh axis runs over, the one named last changes fastest.
Arguments:
- points_x: bfloat16 [32, 524288], P(None, ('leaf', 'sib')), may hold values from -6 to 6
- coords: int32 [2, 524288], P(None, ('leaf', 'sib')), may hold values from 0 to 15, as said below
- near_list: int32 [4096, 9], P(('leaf', 'sib')), may hold values from -1 to 4095, as said below
- leaf_list: int32 [4096, 8], P(('leaf', 'sib')), may hold values from -1 to 4095, as said below
- parent_list: int32 [1024, 27], P(('leaf', 'sib')), may hold values from -1 to 1023, as said below
- basis: bfloat16 [4096, 64, 128], P(('leaf', 'sib')), may hold values from -0.5 to 0.5
- transfer: bfloat16 [1024, 64, 256], P(('leaf', 'sib')), may hold values from -0.375 to 0.375
- leaf_coupling: bfloat16 [4096, 64, 512], P(('leaf', 'sib')), may hold values from -0.25 to 0.25
- parent_coupling: bfloat16 [1024, 64, 1728], P(('leaf', 'sib')), may hold values from -0.15625 to 0.15625
Outputs:
- product: float32 [32, 524288], P(None, ('leaf', 'sib'))
Inputs may be any that keep to these rules, and one draw needn't show every extreme that they name: `coords`: both grid indices of every point lie in 0 to 15. `near_list`: slot k of leaf t is t + (k // 3 - 1) * 128 + k % 3 - 1 or -1; it is -1 where that patch lies outside the grid of rows of 128 leaves; the middle slot is always t. `leaf_list`: each entry is -1 or a leaf of the same aligned group of 512 leaves as t; slot 0 is never -1. `parent_list`: each parent's list holds 1 to 27 valid entries first and -1 after them; some parent has all 27.
All inputs are finite; a program needn't handle non-finite values.
Results may differ from a plain program's by a relative error of at most 0.0023.
Values may be sent and summed in bfloat16 or wider, within the bound.
No kernel may reach another device: no remote copies, remote signals or barrier semaphores. Data moves between devices by JAX's collectives and lax.ppermute only.
A program may use at most 192 MiB of HBM per device.

v0:
```python
import math

import jax
import jax.numpy as jnp
from jax import lax
from jax.sharding import PartitionSpec as P


def extended(x, sides, width):
    for axis, dim in sides:
        size, length = (lax.axis_size(axis), x.shape[dim])
        up = [(i, (i + 1) % size) for i in range(size - 1)]
        down = [(j, i) for i, j in up]
        last = lax.slice_in_dim(x, length - width, length, axis=dim)
        first = lax.slice_in_dim(x, 0, width, axis=dim)
        before = lax.ppermute(last, axis, up)
        after = lax.ppermute(first, axis, down)
        x = jnp.concatenate([before, x, after], axis=dim)
    return x


def couple_rows(lookup, indices, present, blocks, sides, rank_dim):
    count, slots = indices.shape
    safe = jnp.clip(indices, 0, lookup.shape[0] - 1)
    sources = jnp.take(lookup, safe, axis=0)
    sources = jnp.where(present[:, :, None], sources, jnp.zeros_like(sources))
    sources = (
        sources.reshape(count, slots, sides, rank_dim)
        .transpose(0, 2, 1, 3)
        .reshape(count, sides, slots * rank_dim)
    )
    return jnp.einsum("trj,taj->tra", sources, blocks, preferred_element_type=jnp.float32)


def body(
    points_x,
    coords,
    near_list,
    leaf_list,
    parent_list,
    basis,
    transfer,
    leaf_coupling,
    parent_coupling,
):
    sides = points_x.shape[0]
    leaves, rank_dim, leaf_size = basis.shape
    parents = leaves // 4
    point_rows = points_x.reshape(sides, leaves, leaf_size)
    leaf_coef = jnp.einsum(
        "rtl,tal->tra", point_rows, basis, preferred_element_type=jnp.float32
    ).astype(jnp.bfloat16)
    children = (
        leaf_coef.reshape(parents, 4, sides, rank_dim)
        .transpose(0, 2, 1, 3)
        .reshape(parents, sides, 4 * rank_dim)
    )
    parent_coef = jnp.einsum(
        "prj,paj->pra", children, transfer, preferred_element_type=jnp.float32
    ).astype(jnp.bfloat16)
    leaf_flat = leaf_coef.reshape(leaves, sides * rank_dim)
    parent_flat = parent_coef.reshape(parents, sides * rank_dim)
    group_leaf = lax.all_gather(leaf_flat, "sib", axis=0, tiled=True)
    every_parent = lax.all_gather(parent_flat, ("leaf", "sib"), axis=0, tiled=True)
    span = leaves * leaf_size
    wide_x = extended(points_x, ((("leaf", "sib"), 1),), span)
    wide_xy = extended(coords, ((("leaf", "sib"), 1),), span)
    group_base = lax.axis_index("leaf") * (lax.axis_size("sib") * leaves)
    leaf_far = couple_rows(
        group_leaf, leaf_list - group_base, leaf_list >= 0, leaf_coupling, sides, rank_dim
    )
    parent_far = couple_rows(
        every_parent, parent_list, parent_list >= 0, parent_coupling, sides, rank_dim
    ).astype(jnp.bfloat16)
    downward = jnp.einsum("pra,paj->prj", parent_far, transfer, preferred_element_type=jnp.float32)
    downward = (
        downward.reshape(parents, sides, 4, rank_dim)
        .transpose(0, 2, 1, 3)
        .reshape(leaves, sides, rank_dim)
    )
    leaf_total = (leaf_far + downward).astype(jnp.bfloat16)
    far_field = jnp.einsum("tra,tal->rtl", leaf_total, basis, preferred_element_type=jnp.float32)
    target_xy = coords.reshape(2, leaves, leaf_size)
    near_field = jnp.zeros((sides, leaves, leaf_size), jnp.float32)
    for step_y in range(-1, 2):
        row_x = wide_x[:, (step_y + 1) * span : (step_y + 2) * span]
        row_xy = wide_xy[:, (step_y + 1) * span : (step_y + 2) * span]
        padded_x = jnp.pad(row_x, ((0, 0), (leaf_size, leaf_size)))
        padded_xy = jnp.pad(row_xy, ((0, 0), (leaf_size, leaf_size)))
        for step_x in range(-1, 2):
            slot = (step_y + 1) * 3 + (step_x + 1)
            begin = (step_x + 1) * leaf_size
            sources = padded_x[:, begin : begin + span].reshape(sides, leaves, leaf_size)
            source_xy = padded_xy[:, begin : begin + span].reshape(2, leaves, leaf_size)
            delta_x = (target_xy[0][:, :, None] - source_xy[0][:, None, :]).astype(
                jnp.float32
            ) + jnp.float32(-16 * step_x)
            delta_y = (target_xy[1][:, :, None] - source_xy[1][:, None, :]).astype(
                jnp.float32
            ) + jnp.float32(-16 * step_y)
            kernel_block = 4.0 / (math.pi * jnp.sqrt(delta_x * delta_x + delta_y * delta_y + 0.25))
            present = near_list[:, slot] >= 0
            kernel_block = jnp.where(present[:, None, None], kernel_block, jnp.float32(0.0)).astype(
                jnp.bfloat16
            )
            near_field = near_field + jnp.einsum(
                "tij,rtj->rti", kernel_block, sources, preferred_element_type=jnp.float32
            )
    return (far_field + near_field).reshape(sides, leaves * leaf_size)


def solution(mesh):
    in_specs = (
        P(None, ("leaf", "sib")),
        P(None, ("leaf", "sib")),
        P(("leaf", "sib"), None),
        P(("leaf", "sib"), None),
        P(("leaf", "sib"), None),
        P(("leaf", "sib"), None, None),
        P(("leaf", "sib"), None, None),
        P(("leaf", "sib"), None, None),
        P(("leaf", "sib"), None, None),
    )
    out_specs = P(None, ("leaf", "sib"))
    return jax.shard_map(body, mesh=mesh, in_specs=in_specs, out_specs=out_specs, check_vma=False)
```

profile of v0, /device:TPU:0, one launch (start us, length us, event | category | flops | bytes accessed | tf_op | source)
XLA Modules:
  0.0 303.9 jit_solution(13963264469991579623)
XLA Ops:
  6.5 0.0 copy-start
  6.5 1.6 copy-done
  8.1 2.4 convolution_convert_fusion
  10.5 1.9 copy.18
  12.4 2.0 copy.19
  14.5 0.0 all-gather.3.cloned.1.call-update
  14.5 0.0 all-gather.5.cloned.1.call-start
  14.6 5.9 %collective-permute-start = (bf16[32,16384]{1,0:T(8,128)(2,1)}, bf16[32,16384]{1,0:T(8,128)(2,1)}, u32[]{:S(2)}, u32[]{:S(2)}) collective-permute-start(bf16[32,16384]{1,0:T(8,128)(2,1)} %param.9), channel_id=1, source_target_pairs={{0,1},{1,2},{2,3},{3,4},{4,5},{5,6},{6,7},{7,8},{8,9},{9,10},{10,1... | collective-permute-start | bytes 3145736 | tf_op jit(solution)/shard_map/ppermute | solution.py:16
  20.5 2.5 collective-permute-start.1
  23.0 1.3 collective-permute-start.3
  24.3 1.5 collective-permute-start.2
  25.8 1.5 copy.22
  27.3 2.1 reshape.206
  29.4 1.6 convolution_convert_fusion.2
  31.0 0.9 reshape.207
  31.9 0.0 all-gather.5.cloned.1.call-update
  32.0 0.9 pad_slice_fusion.7
  32.9 2.7 slice_bitcast_fusion.3
  35.6 0.7 compare_select_fusion
  36.3 1.3 broadcast_compare_fusion
  37.6 1.6 compare_bitcast_fusion
  39.2 1.3 compare_and_fusion.1
  40.5 0.1 copy.20
  40.6 0.7 reshape.221
  41.3 9.5 %fusion.6 = f32[128,128,32]{1,2,0:T(8,128)} fusion(s32[128,128]{1,0:T(8,128)} %bitcast.158, s32[128,128]{1,0:T(8,128)} %bitcast.167, pred[128]{0:T(512)(128)(4,1)} %get-tuple-element.40, bf16[32,16384]{1,0:T(8,128)(2,1)} %param.9), kind=kOutput, calls=%fused_computation.19 | convolution fusion | flops 159383552 | bytes 3276928 | tf_op jit(solution)/shard_map/tij,rtj->rti/dot_general | solution.py:106
  50.8 0.0 copy-done.2
  50.9 12.8 %fusion.5 = f32[128,32,128]{2,1,0:T(8,128)} fusion(s32[128,128]{1,0:T(8,128)S(1)} %bitcast.181, s32[128,128]{1,0:T(8,128)S(1)} %bitcast.180, s32[128,128]{1,0:T(8,128)S(1)} %bitcast.159, s32[128,128]{1,0:T(8,128)S(1)} %bitcast.168, pred[128]{0:T(512)(128)(4,1)S(1)} %copy-done.21, bf16[4,128,8,128]{3,2,1,0:T(8,128)(2,1)S(1)} %copy-done.2), kind=kOutput, calls=%fused_computation.18 | convolution fusion | flops 161480704 | bytes 3408000 | tf_op jit(solution)/shard_map/tij,rtj->rti/dot_general | solution.py:106
  63.7 0.0 copy-done.9
  63.7 12.8 %fusion.7 = f32[128,32,128]{2,1,0:T(8,128)} fusion(s32[128,128]{1,0:T(8,128)S(1)} %bitcast.179, s32[128,128]{1,0:T(8,128)S(1)} %bitcast.178, s32[128,128]{1,0:T(8,128)S(1)} %bitcast.160, s32[128,128]{1,0:T(8,128)S(1)} %bitcast.169, pred[128]{0:T(512)(128)(4,1)S(1)} %copy-done.20, bf16[4,128,8,128]{3,2,1,0:T(8,128)(2,1)S(1)} %get-tuple-element.16), kind=kOutput, calls=%fused_computation.20 | convolution fusion | flops 161480704 | bytes 3408000 | tf_op jit(solution)/shard_map/tij,rtj->rti/dot_general | solution.py:106
  76.5 0.1 reshape.229
  76.6 0.8 copy.15
  77.4 0.8 copy.16
  78.1 0.0 collective-permute-done.1
  78.2 0.2 pad_slice_fusion.11
  78.4 0.0 collective-permute-done.3
  78.4 0.9 pad_slice_fusion.1
  79.2 0.0 collective-permute-done
  79.2 1.8 slice_bitcast_fusion.5
  81.0 26.6 %collective-permute-done.2 = bf16[32,16384]{1,0:T(8,128)(2,1)} collective-permute-done((bf16[32,16384]{1,0:T(8,128)(2,1)}, bf16[32,16384]{1,0:T(8,128)(2,1)}, u32[]{:S(2)}, u32[]{:S(2)}) %collective-permute-start.2) | collective-permute-done | bytes 1048608 | tf_op jit(solution)/shard_map/ppermute | solution.py:17
  107.6 2.7 slice_bitcast_fusion
  110.3 10.9 %fusion.3 = f32[128,128,32]{1,2,0:T(8,128)} fusion(s32[128,128]{1,0:T(8,128)S(1)} %bitcast.188, s32[128,128]{1,0:T(8,128)S(1)} %bitcast.189, s32[128,128]{1,0:T(8,128)S(1)} %bitcast.161, s32[128,128]{1,0:T(8,128)S(1)} %bitcast.170, pred[128]{0:T(512)(128)(4,1)} %get-tuple-element.43, bf16[32,16384]{1,0:T(8,128)(2,1)} %collective-permute-done), kind=kOutput, calls=%fused_computation.16 | convolution fusion | flops 161480704 | bytes 3408000 | tf_op jit(solution)/shard_map/tij,rtj->rti/dot_general | solution.py:106
  121.3 0.0 copy-done.19
  121.3 0.0 copy-start.18
  121.3 10.9 %fusion.9 = f32[128,128,32]{1,2,0:T(8,128)} fusion(s32[128,128]{1,0:T(8,128)S(1)} %bitcast.190, s32[128,128]{1,0:T(8,128)S(1)} %bitcast.191, s32[128,128]{1,0:T(8,128)S(1)} %bitcast.162, s32[128,128]{1,0:T(8,128)S(1)} %bitcast.171, pred[128]{0:T(512)(128)(4,1)S(1)} %copy-done.19, bf16[32,16384]{1,0:T(8,128)(2,1)} %collective-permute-done.2), kind=kOutput, calls=%fused_computation.22 | convolution fusion | flops 161480704 | bytes 3408000 | tf_op jit(solution)/shard_map/tij,rtj->rti/dot_general | solution.py:106
  132.2 13.2 %fusion.2 = f32[128,32,128]{2,1,0:T(8,128)} fusion(s32[128,128]{1,0:T(8,128)S(1)} %bitcast.187, s32[128,128]{1,0:T(8,128)S(1)} %bitcast.163, s32[128,128]{1,0:T(8,128)S(1)} %bitcast.186, s32[128,128]{1,0:T(8,128)S(1)} %bitcast.172, pred[128]{0:T(512)(128)(4,1)S(1)} %copy-done.18, bf16[4,128,8,128]{3,2,1,0:T(8,128)(2,1)S(1)} %get-tuple-element.13), kind=kOutput, calls=%fused_computation.15 | convolution fusion | flops 163577856 | bytes 3408000 | tf_op jit(solution)/shard_map/tij,rtj->rti/dot_general | solution.py:106
  145.4 13.2 %fusion.4 = f32[128,32,128]{2,1,0:T(8,128)} fusion(s32[128,128]{1,0:T(8,128)S(1)} %bitcast.183, s32[128,128]{1,0:T(8,128)S(1)} %bitcast.182, s32[128,128]{1,0:T(8,128)S(1)} %bitcast.164, s32[128,128]{1,0:T(8,128)S(1)} %bitcast.173, pred[128]{0:T(512)(128)(4,1)S(1)} %copy-done.17, bf16[4,128,8,128]{3,2,1,0:T(8,128)(2,1)S(1)} %get-tuple-element.14), kind=kOutput, calls=%fused_computation.17 | convolution fusion | flops 163577856 | bytes 3408000 | tf_op jit(solution)/shard_map/tij,rtj->rti/dot_general | solution.py:106
  158.6 13.2 %fusion.8 = f32[128,32,128]{2,1,0:T(8,128)} fusion(s32[128,128]{1,0:T(8,128)S(1)} %bitcast.184, s32[128,128]{1,0:T(8,128)S(1)} %bitcast.185, s32[128,128]{1,0:T(8,128)S(1)} %bitcast.165, s32[128,128]{1,0:T(8,128)S(1)} %bitcast.174, pred[128]{0:T(512)(128)(4,1)S(1)} %copy-done.16, bf16[4,128,8,128]{3,2,1,0:T(8,128)(2,1)S(1)} %get-tuple-element.8), kind=kOutput, calls=%fused_computation.21 | convolution fusion | flops 163577856 | bytes 3408000 | tf_op jit(solution)/shard_map/tij,rtj->rti/dot_general | solution.py:106
  171.8 10.7 %gather_fusion = bf16[1024,2048]{1,0:T(8,128)(2,1)} fusion(bf16[512,2048]{1,0:T(8,128)(2,1)} %all-gather.3.cloned.1.call-done, s32[1024]{0:T(1024)S(1)} %broadcast_clamp_fusion), kind=kCustom, calls=%fused_computation | custom fusion | bytes 8392704 | tf_op jit(solution)/shard_map/jit(_take)/gather | solution.py:25
  182.5 12.9 %gather.13 = bf16[128,8,32,64]{3,2,1,0:T(8,128)(2,1)} reshape(bf16[1024,2048]{1,0:T(8,128)(2,1)} %gather_fusion) | data formatting | bytes 8388608 | tf_op jit(solution)/shard_map/jit(_take)/gather | solution.py:25
  195.3 8.1 %select_bitcast_fusion = bf16[128,32,8,64]{3,1,2,0:T(8,128)(2,1)} fusion(bf16[128,8,32,64]{3,2,1,0:T(8,128)(2,1)} %gather.13, pred[128,8]{1,0:T(8,128)(4,1)S(1)} %copy.16, pred[128,8]{1,0:T(8,128)(4,1)S(1)} %copy.15), kind=kLoop, calls=%fused_computation.14 | loop fusion | flops 4194304 | bytes 8390656 | tf_op jit(solution)/shard_map/transpose | solution.py:29
  203.5 11.4 %copy.21 = bf16[128,32,8,64]{0,3,2,1:T(8,128)(2,1)} copy(bf16[128,32,8,64]{3,1,2,0:T(8,128)(2,1)} %select_bitcast_fusion) | data formatting | bytes 8388608 | tf_op jit(solution)/shard_map/transpose | solution.py:29
  214.9 8.0 %copy.34 = bf16[128,32,512]{2,1,0:T(8,128)(2,1)} copy(bf16[128,32,512]{0,2,1:T(8,128)(2,1)} %bitcast.154) | data formatting | bytes 8388608 | tf_op jit(solution)/shard_map/reshape | solution.py:30
  222.8 11.7 %gather_fusion.1 = bf16[864,2048]{1,0:T(8,128)(2,1)} fusion(bf16[1024,2048]{1,0:T(8,128)(2,1)} %all-gather.5.cloned.1.call-done, s32[1024]{0:T(1024)S(1)} %pad_clamp_fusion), kind=kCustom, calls=%fused_computation.1 | custom fusion | bytes 7081344 | tf_op jit(solution)/shard_map/jit(_take)/gather | solution.py:25
  234.5 11.1 %gather.15 = bf16[32,27,32,64]{3,2,1,0:T(8,128)(2,1)} reshape(bf16[864,2048]{1,0:T(8,128)(2,1)} %gather_fusion.1) | data formatting | bytes 7077888 | tf_op jit(solution)/shard_map/jit(_take)/gather | solution.py:25
  245.6 0.0 copy-done.13
  245.6 8.9 %fusion.1 = bf16[32,32,27,64]{3,2,1,0:T(8,128)(2,1)} fusion(bf16[32,27,32,64]{3,2,1,0:T(8,128)(2,1)} %gather.15, pred[32,27]{1,0:T(8,128)(4,1)S(1)} %copy-done.13, pred[32,27]{1,0:T(8,128)(4,1)S(1)} %copy-done.12), kind=kLoop, calls=%fused_computation.4 | loop fusion | flops 3538944 | bytes 7079616 | tf_op jit(solution)/shard_map/transpose | solution.py:29
  254.5 11.6 %reshape.208 = bf16[32,32,1728]{2,1,0:T(8,128)(2,1)} reshape(bf16[32,32,27,64]{3,2,1,0:T(8,128)(2,1)} %fusion.1) | data formatting | bytes 7077888 | tf_op jit(solution)/shard_map/reshape | solution.py:30
  266.1 6.5 %fusion.105 = f32[32,32,256]{2,1,0:T(8,128)S(1)} fusion(bf16[32,64,256]{2,1,0:T(8,128)(2,1)} %param.15, bf16[32,32,1728]{2,1,0:T(8,128)(2,1)} %reshape.208, bf16[32,64,1728]{2,1,0:T(8,128)(2,1)} %param.17), kind=kOutput, calls=%fused_computation.132 | convolution fusion | flops 260112384 | bytes 12713984 | tf_op jit(solution)/shard_map/pra,paj->prj/dot_general | solution.py:75
  272.7 0.4 fusion.172
  273.0 1.5 pad_maximum_fusion
  274.6 9.5 %fusion.104 = f32[128,32,128]{2,1,0:T(8,128)} fusion(bf16[128,64,128]{2,1,0:T(8,128)(2,1)S(1)} %copy-done, f32[128,32,64]{2,1,0:T(8,128)} %bitcast.156, bf16[128,32,512]{2,1,0:T(8,128)(2,1)} %copy.34, bf16[128,64,512]{2,1,0:T(8,128)(2,1)} %param.16), kind=kOutput, calls=%fused_computation.129 | convolution fusion | flops 336068608 | bytes 17825792 | tf_op jit(solution)/shard_map/tra,tal->rtl/dot_general | solution.py:82
  284.1 0.0 copy-done.6
  284.1 11.5 %fusion.103 = f32[128,4,8,128]{3,2,1,0:T(8,128)S(1)} fusion(f32[128,128,32]{1,2,0:T(8,128)} %fusion.9, f32[128,32,128]{2,1,0:T(8,128)} %fusion.8, f32[128,32,128]{2,1,0:T(8,128)} %fusion.7, f32[128,128,32]{1,2,0:T(8,128)} %fusion.6, f32[128,32,128]{2,1,0:T(8,128)} %fusion.5, f32[128,32,128]{2,1,0:T(8,128)} %fusion.4, f32[128,128,32]{1,2,0:T(8,128)} %fusion.3, ...), kind=kOutput, calls=%fused_computation.119 | convolution fusion | flops 168296448 | bytes 22282368 | tf_op jit(solution)/shard_map/tij,rtj->rti/dot_general | solution.py:106
  295.6 1.5 copy.91
  (41 shorter events, 0.1 us)
Async XLA Ops:
  6.5 1.6 copy-start
  6.5 25.4 %copy-start.3 = (s32[2,16384]{1,0:T(2,128)S(1)}, s32[2,16384]{1,0:T(2,128)}, u32[]{:S(2)}) copy-start(s32[2,16384]{1,0:T(2,128)} %param.10) | copy-start | bytes 393220
  6.5 165.2 %all-gather.3.cloned.1.call-start = ((), (), s32[]{:S(2)}) async-start(), calls=%async_computation | async-start | bytes 2621440 | tf_op jit(solution)/shard_map/all_gather | solution.py:63
  14.5 208.3 %all-gather.5.cloned.1.call-start = ((), (), s32[]{:S(2)}) async-start(), calls=%async_computation.1 | async-start | bytes 4325376 | tf_op jit(solution)/shard_map/all_gather | solution.py:64
  14.6 64.7 %collective-permute-start = (bf16[32,16384]{1,0:T(8,128)(2,1)}, bf16[32,16384]{1,0:T(8,128)(2,1)}, u32[]{:S(2)}, u32[]{:S(2)}) collective-permute-start(bf16[32,16384]{1,0:T(8,128)(2,1)} %param.9), channel_id=1, source_target_pairs={{0,1},{1,2},{2,3},{3,4},{4,5},{5,6},{6,7},{7,8},{8,9},{9,10},{10,1... | collective-permute-start | bytes 3145736 | tf_op jit(solution)/shard_map/ppermute | solution.py:16
  20.5 57.7 %collective-permute-start.1 = (s32[2,16384]{1,0:T(2,128)}, s32[2,16384]{1,0:T(2,128)S(1)}, u32[]{:S(2)}, u32[]{:S(2)}) collective-permute-start(s32[2,16384]{1,0:T(2,128)} %param.10), channel_id=1, source_target_pairs={{0,1},{1,2},{2,3},{3,4},{4,5},{5,6},{6,7},{7,8},{8,9},{9,10},{10,1... | collective-permute-start | bytes 393224 | tf_op jit(solution)/shard_map/ppermute | solution.py:16
  23.0 55.4 %collective-permute-start.3 = (s32[2,16384]{1,0:T(2,128)}, s32[2,16384]{1,0:T(2,128)S(1)}, u32[]{:S(2)}, u32[]{:S(2)}) collective-permute-start(s32[2,16384]{1,0:T(2,128)} %param.10), channel_id=1, source_target_pairs={{1,0},{2,1},{3,2},{4,3},{5,4},{6,5},{7,6},{8,7},{9,8},{10,9},{11,1... | collective-permute-start | bytes 393224 | tf_op jit(solution)/shard_map/ppermute | solution.py:17
  24.3 83.3 %collective-permute-start.2 = (bf16[32,16384]{1,0:T(8,128)(2,1)}, bf16[32,16384]{1,0:T(8,128)(2,1)}, u32[]{:S(2)}, u32[]{:S(2)}) collective-permute-start(bf16[32,16384]{1,0:T(8,128)(2,1)} %param.9), channel_id=1, source_target_pairs={{1,0},{2,1},{3,2},{4,3},{5,4},{6,5},{7,6},{8,7},{9,8},{10,9},{11,1... | collective-permute-start | bytes 3145736 | tf_op jit(solution)/shard_map/ppermute | solution.py:17
  41.3 9.5 %copy-start.2 = (bf16[4,128,8,128]{3,2,1,0:T(8,128)(2,1)S(1)}, bf16[4,128,8,128]{3,2,1,0:T(8,128)(2,1)}, u32[]{:S(2)}) copy-start(bf16[4,128,8,128]{3,2,1,0:T(8,128)(2,1)} %get-tuple-element.15) | copy-start | bytes 3145732
  41.3 9.5 %copy-start.4 = (s32[1,16384]{1,0:T(1,128)S(1)}, s32[1,16384]{1,0:T(1,128)}, u32[]{:S(2)}) copy-start(s32[1,16384]{1,0:T(1,128)} %get-tuple-element.33) | copy-start | bytes 196612
  41.3 9.5 %copy-start.5 = (s32[1,16384]{1,0:T(1,128)S(1)}, s32[1,16384]{1,0:T(1,128)}, u32[]{:S(2)}) copy-start(s32[1,16384]{1,0:T(1,128)} %get-tuple-element.34) | copy-start | bytes 196612
  41.3 9.5 %copy-start.10 = (s32[1,16384]{1,0:T(1,128)S(1)}, s32[1,16384]{1,0:T(1,128)}, u32[]{:S(2)}) copy-start(s32[1,16384]{1,0:T(1,128)} %get-tuple-element.29) | copy-start | bytes 196612
  41.3 9.5 %copy-start.11 = (s32[1,16384]{1,0:T(1,128)S(1)}, s32[1,16384]{1,0:T(1,128)}, u32[]{:S(2)}) copy-start(s32[1,16384]{1,0:T(1,128)} %get-tuple-element.30) | copy-start | bytes 196612
  41.3 9.5 %copy-start.21 = (pred[128]{0:T(512)(128)(4,1)S(1)}, pred[128]{0:T(512)(128)(4,1)}, u32[]{:S(2)}) copy-start(pred[128]{0:T(512)(128)(4,1)} %get-tuple-element.41) | copy-start | bytes 388
  50.9 12.8 %copy-start.8 = (s32[1,16384]{1,0:T(1,128)S(1)}, s32[1,16384]{1,0:T(1,128)}, u32[]{:S(2)}) copy-start(s32[1,16384]{1,0:T(1,128)} %get-tuple-element.31) | copy-start | bytes 196612
  50.9 12.8 %copy-start.9 = (s32[1,16384]{1,0:T(1,128)S(1)}, s32[1,16384]{1,0:T(1,128)}, u32[]{:S(2)}) copy-start(s32[1,16384]{1,0:T(1,128)} %get-tuple-element.32) | copy-start | bytes 196612
  50.9 12.8 %copy-start.20 = (pred[128]{0:T(512)(128)(4,1)S(1)}, pred[128]{0:T(512)(128)(4,1)}, u32[]{:S(2)}) copy-start(pred[128]{0:T(512)(128)(4,1)} %get-tuple-element.39) | copy-start | bytes 388
  63.7 12.8 %copy-start.14 = (s32[1024]{0:T(1024)S(1)}, s32[1024]{0:T(1024)}, u32[]{:S(2)}) copy-start(s32[1024]{0:T(1024)} %reshape.221) | copy-start | bytes 12292
  110.3 11.0 %copy-start.19 = (pred[128]{0:T(512)(128)(4,1)S(1)}, pred[128]{0:T(512)(128)(4,1)}, u32[]{:S(2)}) copy-start(pred[128]{0:T(512)(128)(4,1)} %get-tuple-element.45) | copy-start | bytes 388
  121.3 10.9 %copy-start.18 = (pred[128]{0:T(512)(128)(4,1)S(1)}, pred[128]{0:T(512)(128)(4,1)}, u32[]{:S(2)}) copy-start(pred[128]{0:T(512)(128)(4,1)} %get-tuple-element.44) | copy-start | bytes 388
  132.2 13.2 %copy-start.17 = (pred[128]{0:T(512)(128)(4,1)S(1)}, pred[128]{0:T(512)(128)(4,1)}, u32[]{:S(2)}) copy-start(pred[128]{0:T(512)(128)(4,1)} %get-tuple-element.42) | copy-start | bytes 388
  145.4 13.2 %copy-start.16 = (pred[128]{0:T(512)(128)(4,1)S(1)}, pred[128]{0:T(512)(128)(4,1)}, u32[]{:S(2)}) copy-start(pred[128]{0:T(512)(128)(4,1)} %get-tuple-element.38) | copy-start | bytes 388
  234.5 11.1 %copy-start.12 = (pred[32,27]{1,0:T(8,128)(4,1)S(1)}, pred[32,27]{1,0:T(8,128)(4,1)}, u32[]{:S(2)}) copy-start(pred[32,27]{1,0:T(8,128)(4,1)} %get-tuple-element.35) | copy-start | bytes 2596
  234.5 11.1 %copy-start.13 = (pred[32,27]{1,0:T(8,128)(4,1)S(1)}, pred[32,27]{1,0:T(8,128)(4,1)}, u32[]{:S(2)}) copy-start(pred[32,27]{1,0:T(8,128)(4,1)} %get-tuple-element.36) | copy-start | bytes 2596
  274.5 9.5 %copy-start.1 = (bf16[4,128,8,128]{3,2,1,0:T(8,128)(2,1)S(1)}, bf16[4,128,8,128]{3,2,1,0:T(8,128)(2,1)}, u32[]{:S(2)}) copy-start(bf16[4,128,8,128]{3,2,1,0:T(8,128)(2,1)} %get-tuple-element.7) | copy-start | bytes 3145732
  274.5 9.5 %copy-start.6 = (s32[1,16384]{1,0:T(1,128)S(1)}, s32[1,16384]{1,0:T(1,128)}, u32[]{:S(2)}) copy-start(s32[1,16384]{1,0:T(1,128)} %get-tuple-element.17) | copy-start | bytes 196612
  274.5 9.5 %copy-start.7 = (s32[1,16384]{1,0:T(1,128)S(1)}, s32[1,16384]{1,0:T(1,128)}, u32[]{:S(2)}) copy-start(s32[1,16384]{1,0:T(1,128)} %get-tuple-element.19) | copy-start | bytes 196612
  274.5 9.5 %copy-start.15 = (pred[128]{0:T(512)(128)(4,1)S(1)}, pred[128]{0:T(512)(128)(4,1)}, u32[]{:S(2)}) copy-start(pred[128]{0:T(512)(128)(4,1)} %get-tuple-element.37) | copy-start | bytes 388
Sparse Core Ops, SparseCore 0:
  14.6 84.8 all-gather.2
  102.6 60.5 all-gather.4
where the time goes:
time: 306 us; the launch traced here: 304 us
  matrix products  128 us (42%)
  local copies, waits for them, and re-layouts  101 us (33%)
  waiting for transfers between devices  26.7 us (9%)
  other arithmetic  23.5 us (8%)
  between operations  13.7 us (4%)
  starting transfers between devices  11.2 us (4%)
    dot_general x9, matrix products, body(): jnp.einsum('tij,rtj->rti', kernel_block, sources, preferred_element_type=...  108 us
    gather x4, local copies, waits for them, and re-layouts, couple_rows(): sources = jnp.take(lookup, safe, axis=0)  46.3 us
    ppermute x2, waiting for transfers between devices, extended(): after = lax.ppermute(first, axis, down)  26.6 us
    reshape x2, local copies, waits for them, and re-layouts, couple_rows(): sources = sources.reshape(count, slots, sides, rank_dim).transpose(0, 2,...  19.6 us
    transpose x2, other arithmetic, couple_rows(): sources = sources.reshape(count, slots, sides, rank_dim).transpose(0, 2,...  17 us
    transpose x1, local copies, waits for them, and re-layouts, couple_rows(): sources = sources.reshape(count, slots, sides, rank_dim).transpose(0, 2,...  11.4 us
    dot_general x1, matrix products, body(): jnp.einsum('tra,tal->rtl', leaf_total, basis, preferred_element_type=jnp....  9.51 us
    unnamed x47, local copies, waits for them, and re-layouts  8.8 us
  transfers between devices with their start and end apart: 6, of which 1 were waited for; matrix products, arithmetic and copies ran while one was open for 56% of the time, Pallas kernels for 0%

commit v1 on v0

v1 whole, which is shorter than its diff:
```python
import functools
import math

import jax
import jax.numpy as jnp
import numpy as np
from jax import lax
from jax.experimental import pallas as pl
from jax.experimental.pallas import tpu as pltpu
from jax.sharding import PartitionSpec as P

CELLS = 256
NT = (((1,), (1,)), ((), ()))
NN = (((1,), (0,)), ((), ()))
VMEM_LIMIT = 56 * 1024 * 1024


def dot(a, b, dims):
    return lax.dot_general(a, b, dims, preferred_element_type=jnp.float32)


def kernel_table():
    cell = np.arange(CELLS)
    at_x, at_y = cell % 16, cell // 16
    blocks = []
    for step_y in range(-1, 2):
        for step_x in range(-1, 2):
            dx = (at_x[None, :] - at_x[:, None] - 16 * step_x).astype(np.float32)
            dy = (at_y[None, :] - at_y[:, None] - 16 * step_y).astype(np.float32)
            root = np.sqrt(dx * dx + dy * dy + np.float32(0.25))
            blocks.append(np.float32(4.0) / (np.float32(math.pi) * root))
    return np.stack(blocks).reshape(3, 3 * CELLS, CELLS).astype(jnp.bfloat16)


def low_lanes(rows):
    return lax.broadcasted_iota(jnp.int32, (rows, 128), 1) < 64


def one_hot(cells):
    hit = lax.broadcasted_iota(jnp.int32, (CELLS, cells.shape[1]), 0) == cells
    return jnp.where(hit, jnp.float32(1), jnp.float32(0)).astype(jnp.bfloat16)


def split(v):
    high = v.astype(jnp.bfloat16)
    low = (v - high.astype(jnp.float32)).astype(jnp.bfloat16)
    return high, low


def diagonal(y, sides):
    low = low_lanes(sides)
    left = jnp.where(low, y[:sides, :128], y[sides : 2 * sides, :128])
    right = jnp.where(low, y[2 * sides : 3 * sides, 128:], y[3 * sides :, 128:])
    return jnp.concatenate([left, right], axis=1)


def coef_kernel(x_ref, basis_ref, transfer_ref, leaf_ref, parent_ref):
    sides = x_ref.shape[0]
    low = low_lanes(sides)
    for pair in range(leaf_ref.shape[0] // 2):
        rows = []
        for p in (2 * pair, 2 * pair + 1):
            x4 = jnp.concatenate(
                [x_ref[:, (4 * p + c) * 128 : (4 * p + c + 1) * 128] for c in range(4)], axis=0
            )
            y = dot(x4, basis_ref[4 * p : 4 * p + 4].reshape(256, 128), NT)
            coef = diagonal(y, sides).astype(jnp.bfloat16)
            leaf_ref[p] = coef
            rows.append(coef)
        z = dot(
            jnp.concatenate(rows, axis=0),
            transfer_ref[2 * pair : 2 * pair + 2].reshape(128, 256),
            NT,
        )
        parent_ref[pair] = jnp.where(low, z[:sides], z[sides:]).astype(jnp.bfloat16)


def coefficients(x, basis, transfer):
    sides, parents = x.shape[0], transfer.shape[0]
    step = 8
    return pl.pallas_call(
        coef_kernel,
        grid=(parents // step,),
        in_specs=[
            pl.BlockSpec((sides, step * 512), lambda g: (0, g)),
            pl.BlockSpec((step * 4, 64, 128), lambda g: (g, 0, 0)),
            pl.BlockSpec((step, 64, 256), lambda g: (g, 0, 0)),
        ],
        out_specs=[
            pl.BlockSpec((step, sides, 256), lambda g: (g, 0, 0)),
            pl.BlockSpec((step // 2, sides, 128), lambda g: (g, 0, 0)),
        ],
        out_shape=[
            jax.ShapeDtypeStruct((parents, sides, 256), jnp.bfloat16),
            jax.ShapeDtypeStruct((parents // 2, sides, 128), jnp.bfloat16),
        ],
        compiler_params=pltpu.CompilerParams(vmem_limit_bytes=VMEM_LIMIT),
        cost_estimate=pl.CostEstimate(
            flops=600_000_000, bytes_accessed=5_000_000, transcendentals=0
        ),
        name="coefficients",
    )(x, basis, transfer)


def near_kernel(index_ref, x_ref, cells_ref, table_ref, *rest):
    *u_in, u_ref, charge_ref, lhs_ref = rest
    sides = x_ref.shape[0]
    leaves = cells_ref.shape[0]
    step = u_ref.shape[0]
    g = pl.program_id(0)

    @pl.when(g == 0)
    def _():
        charge_ref[leaves] = jnp.zeros(charge_ref.shape[1:], jnp.bfloat16)

        def group(first, carry):
            for extra in range(8):
                t = first * 8 + extra
                hot = one_hot(cells_ref[pl.ds(t, 1), :])
                y = dot(x_ref[:, pl.ds(pl.multiple_of(t * 128, 128), 128)], hot, NT)
                high, low = split(y)
                charge_ref[t, :sides] = high
                charge_ref[t, sides:] = low
            return carry

        lax.fori_loop(0, leaves // 8, group, 0)

    for t in range(step):
        for k in range(3):
            lhs_ref[t * 2 * sides : (t + 1) * 2 * sides, k * CELLS : (k + 1) * CELLS] = charge_ref[
                index_ref[(g * step + t) * 3 + k]
            ]
    u = dot(lhs_ref[...], table_ref[...], NN).reshape(step, 2 * sides, CELLS)
    u = u[:, :sides] + u[:, sides:]
    if u_in:
        u = u + u_in[0][...]
    u_ref[...] = u


def near_row(index, x, cells, table, u=None):
    sides, leaves = x.shape[0], cells.shape[0]
    step = 16
    block = pl.BlockSpec((step, sides, CELLS), lambda g: (g, 0, 0))
    more = [] if u is None else [u]
    return pl.pallas_call(
        near_kernel,
        grid=(leaves // step,),
        in_specs=[
            pl.BlockSpec(memory_space=pltpu.SMEM),
            pl.BlockSpec((sides, leaves * 128), lambda g: (0, 0)),
            pl.BlockSpec((leaves, 128), lambda g: (0, 0)),
            pl.BlockSpec((3 * CELLS, CELLS), lambda g: (0, 0)),
        ]
        + [block] * len(more),
        out_specs=block,
        out_shape=jax.ShapeDtypeStruct((leaves, sides, CELLS), jnp.float32),
        scratch_shapes=[
            pltpu.VMEM((leaves + 1, 2 * sides, CELLS), jnp.bfloat16),
            pltpu.VMEM((step * 2 * sides, 3 * CELLS), jnp.bfloat16),
        ],
        compiler_params=pltpu.CompilerParams(vmem_limit_bytes=VMEM_LIMIT),
        cost_estimate=pl.CostEstimate(
            flops=9_000_000_000, bytes_accessed=8_000_000, transcendentals=0
        ),
        name="near_row",
    )(index, x, cells, table, *more)


def spread(table_ref, at, pair):
    low = low_lanes(pair.shape[0])
    wide = pair.astype(jnp.float32)
    turned = pltpu.roll(wide, 64, 1)
    table_ref[at] = jnp.where(low, wide, turned).astype(jnp.bfloat16)
    table_ref[at + 1] = jnp.where(low, turned, wide).astype(jnp.bfloat16)


def pick(table_ref, first, second):
    low = low_lanes(table_ref.shape[1])
    return jnp.where(low, table_ref[first], table_ref[second])


def parent_kernel(index_ref, pairs_ref, coupling_ref, transfer_ref, down_ref, table_ref, lhs_ref):
    count, sides, _ = down_ref.shape
    slots = coupling_ref.shape[2] // 64
    pairs = pairs_ref.shape[0]
    low = low_lanes(sides)
    g = pl.program_id(0)

    @pl.when(g == 0)
    def _():
        table_ref[2 * pairs] = jnp.zeros(table_ref.shape[1:], jnp.bfloat16)

        def group(first, carry):
            for extra in range(8):
                at = first * 8 + extra
                spread(table_ref, 2 * at, pairs_ref[at])
            return carry

        lax.fori_loop(0, pairs // 8, group, 0)

    for pair in range(count // 2):
        for half in range(2):
            base = (g * count + 2 * pair + half) * slots
            rows = slice(half * sides, (half + 1) * sides)
            for j in range(slots // 2):
                lhs_ref[rows, j * 128 : (j + 1) * 128] = pick(
                    table_ref, index_ref[base + 2 * j], index_ref[base + 2 * j + 1]
                )
            if slots % 2:
                lhs_ref[rows, slots // 2 * 128 :] = table_ref[index_ref[base + slots - 1]]
        y = dot(
            lhs_ref[:, : slots * 64],
            coupling_ref[2 * pair : 2 * pair + 2].reshape(128, slots * 64),
            NT,
        )
        zero = jnp.zeros((sides, 128), jnp.float32)
        own = jnp.concatenate(
            [jnp.where(low, y[:sides], zero), jnp.where(low, zero, y[sides:])], axis=0
        ).astype(jnp.bfloat16)
        d = dot(own, transfer_ref[2 * pair : 2 * pair + 2].reshape(128, 256), NN)
        down_ref[2 * pair] = d[:sides]
        down_ref[2 * pair + 1] = d[sides:]


def parents_down(index, pairs, coupling, transfer):
    parents, _, width = coupling.shape
    sides = pairs.shape[1]
    step = 8
    return pl.pallas_call(
        parent_kernel,
        grid=(parents // step,),
        in_specs=[
            pl.BlockSpec(memory_space=pltpu.SMEM),
            pl.BlockSpec(pairs.shape, lambda g: (0, 0, 0)),
            pl.BlockSpec((step, 64, width), lambda g: (g, 0, 0)),
            pl.BlockSpec((step, 64, 256), lambda g: (g, 0, 0)),
        ],
        out_specs=pl.BlockSpec((step, sides, 256), lambda g: (g, 0, 0)),
        out_shape=jax.ShapeDtypeStruct((parents, sides, 256), jnp.float32),
        scratch_shapes=[
            pltpu.VMEM((2 * pairs.shape[0] + 1, sides, 128), jnp.bfloat16),
            pltpu.VMEM((2 * sides, (width + 127) // 128 * 128), jnp.bfloat16),
        ],
        compiler_params=pltpu.CompilerParams(vmem_limit_bytes=VMEM_LIMIT),
        cost_estimate=pl.CostEstimate(
            flops=4_000_000_000, bytes_accessed=14_000_000, transcendentals=0
        ),
        name="parents_down",
    )(index, pairs, coupling, transfer)


def final_kernel(pieces, index_ref, *rest):
    piece_refs = rest[:pieces]
    coupling_ref, down_ref, basis_ref, cells_ref, u_ref, out_ref, table_ref, lhs_ref = rest[pieces:]
    parents, sides, _ = down_ref.shape
    slots = coupling_ref.shape[2] // 64
    per_piece = piece_refs[0].shape[0]
    g = pl.program_id(0)

    @pl.when(g == 0)
    def _():
        table_ref[4 * pieces * per_piece] = jnp.zeros(table_ref.shape[1:], jnp.bfloat16)
        for number, piece_ref in enumerate(piece_refs):

            def group(first, carry):
                for extra in range(4):
                    p = first * 4 + extra
                    row = piece_ref[p]
                    at = (number * per_piece + p) * 4
                    spread(table_ref, at, row[:, :128])
                    spread(table_ref, at + 2, row[:, 128:])
                return carry

            lax.fori_loop(0, per_piece // 4, group, 0)

    low = low_lanes(sides)
    for p in range(parents):
        for c in range(4):
            base = (g * parents * 4 + 4 * p + c) * slots
            for j in range(slots // 2):
                lhs_ref[c * sides : (c + 1) * sides, j * 128 : (j + 1) * 128] = pick(
                    table_ref, index_ref[base + 2 * j], index_ref[base + 2 * j + 1]
                )
        y = dot(lhs_ref[...], coupling_ref[4 * p : 4 * p + 4].reshape(256, slots * 64), NT)
        total = diagonal(y, sides) + down_ref[p]
        left, right = total[:, :128], total[:, 128:]
        zero = jnp.zeros((sides, 128), jnp.float32)
        own = jnp.concatenate(
            [
                jnp.concatenate([jnp.where(low, left, zero), zero], axis=1),
                jnp.concatenate([jnp.where(low, zero, left), zero], axis=1),
                jnp.concatenate([zero, jnp.where(low, right, zero)], axis=1),
                jnp.concatenate([zero, jnp.where(low, zero, right)], axis=1),
            ],
            axis=0,
        ).astype(jnp.bfloat16)
        far = dot(own, basis_ref[4 * p : 4 * p + 4].reshape(256, 128), NN)
        for c in range(4):
            t = 4 * p + c
            hot = one_hot(cells_ref[t : t + 1, :])
            near = dot(jnp.concatenate(split(u_ref[t]), axis=0), hot, NN)
            out_ref[:, t * 128 : (t + 1) * 128] = (
                far[c * sides : (c + 1) * sides] + near[:sides] + near[sides:]
            )


def finish(index, pieces, coupling, down, basis, cells, u):
    leaves, _, width = coupling.shape
    sides = down.shape[1]
    step = 16
    whole = pl.BlockSpec(pieces[0].shape, lambda g: (0, 0, 0))
    return pl.pallas_call(
        functools.partial(final_kernel, len(pieces)),
        grid=(leaves // step,),
        in_specs=[pl.BlockSpec(memory_space=pltpu.SMEM)]
        + [whole] * len(pieces)
        + [
            pl.BlockSpec((step, 64, width), lambda g: (g, 0, 0)),
            pl.BlockSpec((step // 4, sides, 256), lambda g: (g, 0, 0)),
            pl.BlockSpec((step, 64, 128), lambda g: (g, 0, 0)),
            pl.BlockSpec((step, 128), lambda g: (g, 0)),
            pl.BlockSpec((step, sides, CELLS), lambda g: (g, 0, 0)),
        ],
        out_specs=pl.BlockSpec((sides, step * 128), lambda g: (0, g)),
        out_shape=jax.ShapeDtypeStruct((sides, leaves * 128), jnp.float32),
        scratch_shapes=[
            pltpu.VMEM((len(pieces) * leaves + 1, sides, 128), jnp.bfloat16),
            pltpu.VMEM((4 * sides, width), jnp.bfloat16),
        ],
        compiler_params=pltpu.CompilerParams(vmem_limit_bytes=VMEM_LIMIT),
        cost_estimate=pl.CostEstimate(
            flops=6_000_000_000, bytes_accessed=20_000_000, transcendentals=0
        ),
        name="finish",
    )(index, *pieces, coupling, down, basis, cells, u)


def body(
    points_x,
    coords,
    near_list,
    leaf_list,
    parent_list,
    basis,
    transfer,
    leaf_coupling,
    parent_coupling,
):
    sides = points_x.shape[0]
    leaves, rank_dim, leaf_size = basis.shape
    parents = leaves // 4
    everyone = ("leaf", "sib")
    devices = lax.axis_size("leaf") * lax.axis_size("sib")
    sibs = lax.axis_size("sib")
    table = jnp.asarray(kernel_table())

    packed_xy = coords.astype(jnp.bfloat16).reshape(sides, -1)
    packed = jnp.concatenate([points_x, packed_xy], axis=1)
    upward = [(i, i + 1) for i in range(devices - 1)]
    downward = [(j, i) for i, j in upward]
    before = lax.ppermute(packed, everyone, upward)
    after = lax.ppermute(packed, everyone, downward)

    leaf_coef, parent_pairs = coefficients(points_x, basis, transfer)
    every_parent = lax.all_gather(parent_pairs, everyone, axis=0, tiled=True)
    pieces = [leaf_coef]
    for shift in range(1, sibs):
        turn = [(i, (i + shift) % sibs) for i in range(sibs)]
        pieces.append(lax.ppermute(leaf_coef, "sib", turn))

    own_cells = (coords[1] * 16 + coords[0]).reshape(leaves, leaf_size)

    def cells_of(other):
        xy = other[:, leaves * leaf_size :].astype(jnp.int32).reshape(2, leaves, leaf_size)
        return xy[1] * 16 + xy[0]

    leaf_ids = jnp.arange(leaves, dtype=jnp.int32)[:, None]
    steps = jnp.arange(3, dtype=jnp.int32)[None, :] - 1
    near_index = jnp.where(
        near_list.reshape(leaves, 3, 3) >= 0, (leaf_ids + steps)[:, None, :], leaves
    )

    def row_index(row):
        return near_index[:, row].reshape(-1)

    me = lax.axis_index("sib")
    group_base = lax.axis_index("leaf") * (sibs * leaves)
    local = leaf_list - group_base
    piece = jnp.bitwise_and(me - local // leaves + sibs, sibs - 1)
    leaf_index = jnp.where(leaf_list >= 0, piece * leaves + local % leaves, sibs * leaves)
    parent_index = jnp.where(parent_list >= 0, parent_list, parents * devices)

    u = near_row(row_index(1), points_x, own_cells, table[1])
    u = near_row(row_index(0), before[:, : leaves * leaf_size], cells_of(before), table[0], u)
    u = near_row(row_index(2), after[:, : leaves * leaf_size], cells_of(after), table[2], u)
    down = parents_down(parent_index.reshape(-1), every_parent, parent_coupling, transfer)
    return finish(
        leaf_index.reshape(-1), pieces, leaf_coupling, down, basis, own_cells, u
    )


def solution(mesh):
    in_specs = (
        P(None, ("leaf", "sib")),
        P(None, ("leaf", "sib")),
        P(("leaf", "sib"), None),
        P(("leaf", "sib"), None),
        P(("leaf", "sib"), None),
        P(("leaf", "sib"), None, None),
        P(("leaf", "sib"), None, None),
        P(("leaf", "sib"), None, None),
        P(("leaf", "sib"), None, None),
    )
    out_specs = P(None, ("leaf", "sib"))
    return jax.shard_map(body, mesh=mesh, in_specs=in_specs, out_specs=out_specs, check_vma=False)
```

time: 306 us -> 174 us (0.57)
  matrix products: 128 us -> 0 us
  local copies, waits for them, and re-layouts: 101 us -> 11.1 us
  Pallas kernels: 0 us -> 79.6 us
  waiting for transfers between devices: 26.7 us -> 53.9 us
  other arithmetic: 23.5 us -> 1.57 us
    dot_general x13 -> x0, matrix products: 128 us -> none  [the longest x9 108 us: body(): jnp.einsum('tij,rtj->rti', kernel_block, sources, preferred_element_type=...]
    pallas_call x0 -> x6, Pallas kernels: none -> 79.6 us  [the longest x3 40.3 us: near_row(): pl.pallas_call(near_kernel, grid=(leaves // step,), in_specs=[pl.BlockSpe...]
    gather x4 -> x0, local copies, waits for them, and re-layouts: 46.3 us -> none  [couple_rows(): sources = jnp.take(lookup, safe, axis=0)]
    reshape x6 -> x3, local copies, waits for them, and re-layouts: 26.1 us -> 1.4 us  [the longest x1 0.69 us: body(): parent_index.reshape(-1)]
    all_gather x2 -> x1, waiting for transfers between devices: 0.01 us -> 23.8 us  [body(): every_parent = lax.all_gather(parent_pairs, everyone, axis=0, tiled=True)]
    transpose x2 -> x0, other arithmetic: 17 us -> none  [couple_rows(): sources = sources.reshape(count, slots, sides, rank_dim).transpose(0, 2,...]
    transpose x2 -> x0, local copies, waits for them, and re-layouts: 12.9 us -> none  [the longest x1 11.4 us: couple_rows(): sources = sources.reshape(count, slots, sides, rank_dim).transpose(0, 2,...]
    unnamed x47 -> x7, local copies, waits for them, and re-layouts: 8.8 us -> 1.34 us
  transfers between devices with their start and end apart: 6 -> 6, of which waited for: 1 -> 2; matrix products, arithmetic and copies ran while one was open for 56% -> 7% of each run, Pallas kernels for 0% -> 36%
where the time goes in v1:
time: 174 us; the launch traced here: 173 us
  Pallas kernels  79.6 us (46%)
  waiting for transfers between devices  53.9 us (31%)
  between operations  13.5 us (8%)
  starting transfers between devices  12.8 us (7%)
  local copies, waits for them, and re-layouts  11.1 us (6%)
    pallas_call x3, Pallas kernels, near_row(): pl.pallas_call(near_kernel, grid=(leaves // step,), in_specs=[pl.BlockSpe...  40.3 us
    ppermute x1, waiting for transfers between devices, body(): after = lax.ppermute(packed, everyone, downward)  30.1 us
    all_gather x1, waiting for transfers between devices, body(): every_parent = lax.all_gather(parent_pairs, everyone, axis=0, tiled=True)  23.8 us
    pallas_call x1, Pallas kernels, finish(): pl.pallas_call(functools.partial(final_kernel, len(pieces)), grid=(leaves...  17.8 us
    pallas_call x1, Pallas kernels, parents_down(): pl.pallas_call(parent_kernel, grid=(parents // step,), in_specs=[pl.Block...  16 us
    ppermute x3, starting transfers between devices, body(): pieces.append(lax.ppermute(leaf_coef, 'sib', turn))  6.52 us
    pallas_call x1, Pallas kernels, coefficients(): pl.pallas_call(coef_kernel, grid=(parents // step,), in_specs=[pl.BlockSp...  5.51 us
    ppermute x1, starting transfers between devices, body(): before = lax.ppermute(packed, everyone, upward)  5 us
  transfers between devices with their start and end apart: 6, of which 2 were waited for; matrix products, arithmetic and copies ran while one was open for 7% of the time, Pallas kernels for 36%

profile of v1, /device:TPU:0, one launch (start us, length us, event | category | flops | bytes accessed | tf_op | source)
XLA Modules:
  0.0 172.6 jit_solution(13232979423743217988)
XLA Ops:
  6.5 0.0 copy-start
  6.5 0.0 all-gather.2.cloned.1.call-start
  6.5 1.3 constant_dynamic-update-slice_fusion.1
  7.9 0.0 copy-done
  8.0 0.0 copy-start.2
  8.0 5.0 %collective-permute-start.4 = (bf16[32,17408]{1,0:T(8,128)(2,1)S(1)}, bf16[32,17408]{1,0:T(8,128)(2,1)S(1)}, u32[]{:S(2)}, u32[]{:S(2)}) collective-permute-start(bf16[32,17408]{1,0:T(8,128)(2,1)S(1)} %constant_dynamic-update-slice_fusion), channel_id=1, source_target_pairs={{0,1},{1,2},{2,3},{3,4},{4,5},{5,6},{6,7},{7,8},{8,9},{9,10},{10,1... | collective-permute-start | bytes 3342344 | tf_op jit(solution)/shard_map/ppermute | solution.py:361
  13.0 1.3 collective-permute-start.3
  14.3 5.5 %coefficients.1 = (bf16[32,32,256]{2,1,0:T(8,128)(2,1)}, bf16[16,32,128]{2,1,0:T(8,128)(2,1)}) custom-call(bf16[32,16384]{1,0:T(8,128)(2,1)} %x_ref.3, bf16[128,64,128]{2,1,0:T(8,128)(2,1)} %rest_6_.1, bf16[32,64,256]{2,1,0:T(8,128)(2,1)} %transfer_ref.3), custom_call_target="tpu_custom_call" | custom-call | flops 600000000 | bytes 5000000 | tf_op jit(solution)/shard_map/coefficients/pallas_call | solution.py:81
  19.8 0.0 copy-start.1
  19.8 2.6 %collective-permute-start = (bf16[32,32,256]{2,1,0:T(8,128)(2,1)}, bf16[32,32,256]{2,1,0:T(8,128)(2,1)}, u32[]{:S(2)}, u32[]{:S(2)}) collective-permute-start(bf16[32,32,256]{2,1,0:T(8,128)(2,1)} %get-tuple-element.7.rest_0_), channel_id=1, source_target_pairs={{0,1},{1,2},{2,3},{3,0},{4,5},{5,6},{6,7},{7,4},{8,9},{9,10},{10,1... | collective-permute-start | bytes 1572872 | tf_op jit(solution)/shard_map/ppermute | solution.py:369
  22.5 2.5 %collective-permute-start.1 = (bf16[32,32,256]{2,1,0:T(8,128)(2,1)}, bf16[32,32,256]{2,1,0:T(8,128)(2,1)}, u32[]{:S(2)}, u32[]{:S(2)}) collective-permute-start(bf16[32,32,256]{2,1,0:T(8,128)(2,1)} %get-tuple-element.7.rest_0_), channel_id=1, source_target_pairs={{0,2},{1,3},{2,0},{3,1},{4,6},{5,7},{6,4},{7,5},{8,10},{9,11},{10,... | collective-permute-start | bytes 1572872 | tf_op jit(solution)/shard_map/ppermute | solution.py:369
  25.0 1.3 collective-permute-start.2
  26.3 0.0 all-gather.2.cloned.1.call-update
  26.4 0.0 copy-done.2
  26.4 0.2 copy.14
  26.7 0.6 fusion.10
  27.3 0.7 slice_add_fusion.2
  28.0 0.7 fusion.5
  28.7 1.6 reshape_squeeze.11.index_ref
  30.3 1.6 reshape_squeeze.10.index_ref
  31.9 0.8 reshape_squeeze.9.index_ref
  32.7 0.1 copy.13
  32.8 0.7 reshape.56.index_ref
  33.5 0.0 copy-done.1
  33.5 0.7 reshape.57.index_ref
  34.2 12.5 %near_row.3.rest_0_ = f32[128,32,256]{2,1,0:T(8,128)} custom-call(s32[384]{0:T(512)} %reshape_squeeze.11.index_ref, bf16[32,16384]{1,0:T(8,128)(2,1)} %x_ref.3, s32[128,128]{1,0:T(8,128)} %bitcast.9, bf16[768,256]{1,0:T(8,128)(2,1)} %constant.62.table_ref), custom_call_target="tpu_custom_call" | custom-call | flops 8999999488 | bytes 8000000 | tf_op jit(solution)/shard_map/near_row/pallas_call | solution.py:145
  46.7 0.0 collective-permute-done.4
  46.7 0.6 add.68.cells_ref
  47.3 30.1 %collective-permute-done.3 = bf16[32,17408]{1,0:T(8,128)(2,1)S(1)} collective-permute-done((bf16[32,17408]{1,0:T(8,128)(2,1)S(1)}, bf16[32,17408]{1,0:T(8,128)(2,1)S(1)}, u32[]{:S(2)}, u32[]{:S(2)}) %collective-permute-start.3) | collective-permute-done | bytes 1114144 | tf_op jit(solution)/shard_map/ppermute | solution.py:362
  77.5 0.6 add.66.cells_ref
  78.1 1.1 slice.74.x_ref
  79.2 1.0 slice.69.x_ref
  80.3 13.9 %near_row.4.rest_0_ = f32[128,32,256]{2,1,0:T(8,128)} custom-call(s32[384]{0:T(512)} %reshape_squeeze.10.index_ref, bf16[32,16384]{1,0:T(8,128)(2,1)} %slice.74.x_ref, s32[128,128]{1,0:T(8,128)} %add.68.cells_ref, bf16[768,256]{1,0:T(8,128)(2,1)} %constant.60.table_ref, f32[128,32,256]{2,1,0:T(8,128)} %near_row.3.rest_0_), custom_call_target="tpu_custom_call" | custom-call | flops 8999999488 | bytes 8000000 | tf_op jit(solution)/shard_map/near_row/pallas_call | solution.py:145
  94.1 13.9 %near_row.5.rest_8_ = f32[128,32,256]{2,1,0:T(8,128)} custom-call(s32[384]{0:T(512)} %reshape_squeeze.9.index_ref, bf16[32,16384]{1,0:T(8,128)(2,1)} %slice.69.x_ref, s32[128,128]{1,0:T(8,128)} %add.66.cells_ref, bf16[768,256]{1,0:T(8,128)(2,1)} %constant.58.table_ref, f32[128,32,256]{2,1,0:T(8,128)} %near_row.4.rest_0_), custom_call_target="tpu_custom_call" | custom-call | flops 8999999488 | bytes 8000000 | tf_op jit(solution)/shard_map/near_row/pallas_call | solution.py:145
  108.1 23.8 %all-gather.2.cloned.1.call-done.pairs_ref = bf16[512,32,128]{2,1,0:T(8,128)(2,1)} async-done(((bf16[16,32,128]{2,1,0:T(8,128)(2,1)}), bf16[512,32,128]{2,1,0:T(8,128)(2,1)}) %all-gather.2.cloned.1.call-update) | async-done | bytes 4194320 | tf_op jit(solution)/shard_map/all_gather | solution.py:365
  131.9 16.0 %parents_down.1.rest_5_ = f32[32,32,256]{2,1,0:T(8,128)} custom-call(s32[864]{0:T(1024)} %reshape.57.index_ref, bf16[512,32,128]{2,1,0:T(8,128)(2,1)} %all-gather.2.cloned.1.call-done.pairs_ref, bf16[32,64,1728]{2,1,0:T(8,128)(2,1)} %coupling_ref.1, bf16[32,64,256]{2,1,0:T(8,128)(2,1)} %transfer_ref.3), custom_call_target="tpu_custom_call" | custom-call | flops 4000000000 | bytes 14000000 | tf_op jit(solution)/shard_map/parents_down/pallas_call | solution.py:229
  147.9 0.0 collective-permute-done.rest_1_
  147.9 0.0 collective-permute-done.1.rest_2_
  147.9 0.0 collective-permute-done.2.rest_3_
  147.9 17.8 %finish.1 = f32[32,16384]{1,0:T(8,128)} custom-call(s32[1024]{0:T(1024)} %reshape.56.index_ref, bf16[32,32,256]{2,1,0:T(8,128)(2,1)} %get-tuple-element.7.rest_0_, bf16[32,32,256]{2,1,0:T(8,128)(2,1)} %collective-permute-done.rest_1_, bf16[32,32,256]{2,1,0:T(8,128)(2,1)} %collective-permute-done.1.rest_2_, ...), custom_call_target="tpu_custom_call" | custom-call | flops 6000000000 | bytes 20000000 | tf_op jit(solution)/shard_map/finish/pallas_call | solution.py:312
  (13 shorter events, 0.2 us)
Async XLA Ops:
  6.5 1.3 copy-start
  6.5 125.3 %all-gather.2.cloned.1.call-start = ((), (), s32[]{:S(2)}) async-start(), calls=%async_computation | async-start | bytes 4325376 | tf_op jit(solution)/shard_map/all_gather | solution.py:365
  8.0 18.4 %copy-start.2 = (s32[128,9]{0,1:T(8,128)S(1)}, s32[128,9]{0,1:T(8,128)}, u32[]{:S(2)}) copy-start(s32[128,9]{0,1:T(8,128)} %param.12) | copy-start | bytes 13828
  8.0 38.7 %collective-permute-start.4 = (bf16[32,17408]{1,0:T(8,128)(2,1)S(1)}, bf16[32,17408]{1,0:T(8,128)(2,1)S(1)}, u32[]{:S(2)}, u32[]{:S(2)}) collective-permute-start(bf16[32,17408]{1,0:T(8,128)(2,1)S(1)} %constant_dynamic-update-slice_fusion), channel_id=1, source_target_pairs={{0,1},{1,2},{2,3},{3,4},{4,5},{5,6},{6,7},{7,8},{8,9},{9,10},{10,1... | collective-permute-start | bytes 3342344 | tf_op jit(solution)/shard_map/ppermute | solution.py:361
  13.0 64.4 %collective-permute-start.3 = (bf16[32,17408]{1,0:T(8,128)(2,1)S(1)}, bf16[32,17408]{1,0:T(8,128)(2,1)S(1)}, u32[]{:S(2)}, u32[]{:S(2)}) collective-permute-start(bf16[32,17408]{1,0:T(8,128)(2,1)S(1)} %constant_dynamic-update-slice_fusion), channel_id=1, source_target_pairs={{1,0},{2,1},{3,2},{4,3},{5,4},{6,5},{7,6},{8,7},{9,8},{10,9},{11,1... | collective-permute-start | bytes 3342344 | tf_op jit(solution)/shard_map/ppermute | solution.py:362
  19.8 13.7 %copy-start.1 = (s32[32,27]{1,0:T(8,128)S(1)}, s32[32,27]{1,0:T(8,128)}, u32[]{:S(2)}) copy-start(s32[32,27]{1,0:T(8,128)} %param.14) | copy-start | bytes 10372
  19.8 128.1 %collective-permute-start = (bf16[32,32,256]{2,1,0:T(8,128)(2,1)}, bf16[32,32,256]{2,1,0:T(8,128)(2,1)}, u32[]{:S(2)}, u32[]{:S(2)}) collective-permute-start(bf16[32,32,256]{2,1,0:T(8,128)(2,1)} %get-tuple-element.7.rest_0_), channel_id=1, source_target_pairs={{0,1},{1,2},{2,3},{3,0},{4,5},{5,6},{6,7},{7,4},{8,9},{9,10},{10,1... | collective-permute-start | bytes 1572872 | tf_op jit(solution)/shard_map/ppermute | solution.py:369
  22.5 125.5 %collective-permute-start.1 = (bf16[32,32,256]{2,1,0:T(8,128)(2,1)}, bf16[32,32,256]{2,1,0:T(8,128)(2,1)}, u32[]{:S(2)}, u32[]{:S(2)}) collective-permute-start(bf16[32,32,256]{2,1,0:T(8,128)(2,1)} %get-tuple-element.7.rest_0_), channel_id=1, source_target_pairs={{0,2},{1,3},{2,0},{3,1},{4,6},{5,7},{6,4},{7,5},{8,10},{9,11},{10,... | collective-permute-start | bytes 1572872 | tf_op jit(solution)/shard_map/ppermute | solution.py:369
  25.0 122.9 %collective-permute-start.2 = (bf16[32,32,256]{2,1,0:T(8,128)(2,1)}, bf16[32,32,256]{2,1,0:T(8,128)(2,1)}, u32[]{:S(2)}, u32[]{:S(2)}) collective-permute-start(bf16[32,32,256]{2,1,0:T(8,128)(2,1)} %get-tuple-element.7.rest_0_), channel_id=1, source_target_pairs={{0,3},{1,0},{2,1},{3,2},{4,7},{5,4},{6,5},{7,6},{8,11},{9,8},{10,9... | collective-permute-start | bytes 1572872 | tf_op jit(solution)/shard_map/ppermute | solution.py:369
Sparse Core Ops, SparseCore 0:
  26.5 105.3 all-gather.1

commit v2 on v1

--- a/solution.py
+++ b/solution.py
@@ -96,74 +96,128 @@
         ],
         compiler_params=pltpu.CompilerParams(vmem_limit_bytes=VMEM_LIMIT),
         cost_estimate=pl.CostEstimate(
-            flops=600_000_000, bytes_accessed=5_000_000, transcendentals=0
+            flops=1000000, bytes_accessed=1000, transcendentals=0
         ),
         name="coefficients",
     )(x, basis, transfer)
 
 
-def near_kernel(index_ref, x_ref, cells_ref, table_ref, *rest):
-    *u_in, u_ref, charge_ref, lhs_ref = rest
+def scatter_row(charge_ref, base, x_ref, cells_ref):
     sides = x_ref.shape[0]
-    leaves = cells_ref.shape[0]
-    step = u_ref.shape[0]
+
+    def group(first, carry):
+        for extra in range(8):
+            t = first * 8 + extra
+            hot = one_hot(cells_ref[pl.ds(t, 1), :])
+            y = dot(x_ref[:, pl.ds(pl.multiple_of(t * 128, 128), 128)], hot, NT)
+            high, low = split(y)
+            charge_ref[base + t, :sides] = high
+            charge_ref[base + t, sides:] = low
+        return carry
+
+    lax.fori_loop(0, cells_ref.shape[0] // 8, group, 0)
+
+
+def grid_field(index_ref, charge_ref, lhs_ref, table_ref, first, step):
+    sides = charge_ref.shape[1] // 2
+    slots = table_ref.shape[0] // CELLS
+    for t in range(step):
+        for k in range(slots):
+            lhs_ref[t * 2 * sides : (t + 1) * 2 * sides, k * CELLS : (k + 1) * CELLS] = charge_ref[
+                index_ref[(first + t) * slots + k]
+            ]
+    u = dot(lhs_ref[...], table_ref[...], NN).reshape(step, 2 * sides, CELLS)
+    return u[:, :sides] + u[:, sides:]
+
+
+def near_own_kernel(index_ref, x_ref, cells_ref, table_ref, u_ref, charge_ref, lhs_ref):
+    leaves, step = cells_ref.shape[0], u_ref.shape[0]
     g = pl.program_id(0)
 
     @pl.when(g == 0)
     def _():
         charge_ref[leaves] = jnp.zeros(charge_ref.shape[1:], jnp.bfloat16)
-
-        def group(first, carry):
-            for extra in range(8):
-                t = first * 8 + extra
-                hot = one_hot(cells_ref[pl.ds(t, 1), :])
-                y = dot(x_ref[:, pl.ds(pl.multiple_of(t * 128, 128), 128)], hot, NT)
-                high, low = split(y)
-                charge_ref[t, :sides] = high
-                charge_ref[t, sides:] = low
-            return carry
-
-        lax.fori_loop(0, leaves // 8, group, 0)
-
-    for t in range(step):
-        for k in range(3):
-            lhs_ref[t * 2 * sides : (t + 1) * 2 * sides, k * CELLS : (k + 1) * CELLS] = charge_ref[
-                index_ref[(g * step + t) * 3 + k]
-            ]
-    u = dot(lhs_ref[...], table_ref[...], NN).reshape(step, 2 * sides, CELLS)
-    u = u[:, :sides] + u[:, sides:]
-    if u_in:
-        u = u + u_in[0][...]
-    u_ref[...] = u
-
-
-def near_row(index, x, cells, table, u=None):
+        scatter_row(charge_ref, 0, x_ref, cells_ref)
+
+    u_ref[...] = grid_field(index_ref, charge_ref, lhs_ref, table_ref, g * step, step)
+
+
+def near_own(index, x, cells, table):
     sides, leaves = x.shape[0], cells.shape[0]
     step = 16
-    block = pl.BlockSpec((step, sides, CELLS), lambda g: (g, 0, 0))
-    more = [] if u is None else [u]
     return pl.pallas_call(
-        near_kernel,
+        near_own_kernel,
         grid=(leaves // step,),
         in_specs=[
             pl.BlockSpec(memory_space=pltpu.SMEM),
             pl.BlockSpec((sides, leaves * 128), lambda g: (0, 0)),
             pl.BlockSpec((leaves, 128), lambda g: (0, 0)),
-            pl.BlockSpec((3 * CELLS, CELLS), lambda g: (0, 0)),
-        ]
-        + [block] * len(more),
-        out_specs=block,
+            pl.BlockSpec(table.shape, lambda g: (0, 0)),
+        ],
+        out_specs=pl.BlockSpec((step, sides, CELLS), lambda g: (g, 0, 0)),
         out_shape=jax.ShapeDtypeStruct((leaves, sides, CELLS), jnp.float32),
         scratch_shapes=[
             pltpu.VMEM((leaves + 1, 2 * sides, CELLS), jnp.bfloat16),
-            pltpu.VMEM((step * 2 * sides, 3 * CELLS), jnp.bfloat16),
+            pltpu.VMEM((step * 2 * sides, table.shape[0]), jnp.bfloat16),
         ],
         compiler_params=pltpu.CompilerParams(vmem_limit_bytes=VMEM_LIMIT),
         cost_estimate=pl.CostEstimate(
-            flops=9_000_000_000, bytes_accessed=8_000_000, transcendentals=0
+            flops=1000000, bytes_accessed=1000, transcendentals=0
         ),
-        name="near_row",
-    )(index, x, cells, table, *more)
+        name="near_own",
+    )(index, x, cells, table)
+
+
+def near_rest_kernel(
+    index_ref, above_ref, below_ref, cells_above_ref, cells_below_ref, table_ref, cells_ref, u_ref, out_ref, charge_ref, lhs_ref
+):
+    leaves, step = cells_above_ref.shape[0], u_ref.shape[0]
+    sides = u_ref.shape[1]
+    g = pl.program_id(0)
+
+    @pl.when(g == 0)
+    def _():
+        charge_ref[2 * leaves] = jnp.zeros(charge_ref.shape[1:], jnp.bfloat16)
+        scatter_row(charge_ref, 0, above_ref, cells_above_ref)
+        scatter_row(charge_ref, leaves, below_ref, cells_below_ref)
+
+    u = u_ref[...] + grid_field(index_ref, charge_ref, lhs_ref, table_ref, g * step, step)
+    for t in range(step):
+        hot = one_hot(cells_ref[t : t + 1, :])
+        near = dot(jnp.concatenate(split(u[t]), axis=0), hot, NN)
+        out_ref[:, t * 128 : (t + 1) * 128] = near[:sides] + near[sides:]
+
+
+def near_rest(index, above, below, cells_above, cells_below, table, cells, u):
+    leaves, sides, _ = u.shape
+    step = 16
+    row = pl.BlockSpec((sides, leaves * 128), lambda g: (0, 0))
+    row_cells = pl.BlockSpec((leaves, 128), lambda g: (0, 0))
+    return pl.pallas_call(
+        near_rest_kernel,
+        grid=(leaves // step,),
+        in_specs=[
+            pl.BlockSpec(memory_space=pltpu.SMEM),
+            row,
+            row,
+            row_cells,
+            row_cells,
+            pl.BlockSpec(table.shape, lambda g: (0, 0)),
+            pl.BlockSpec((step, 128), lambda g: (g, 0)),
+            pl.BlockSpec((step, sides, CELLS), lambda g: (g, 0, 0)),
+        ],
+        out_specs=pl.BlockSpec((sides, step * 128), lambda g: (0, g)),
+        out_shape=jax.ShapeDtypeStruct((sides, leaves * 128), jnp.float32),
+        scratch_shapes=[
+            pltpu.VMEM((2 * leaves + 1, 2 * sides, CELLS), jnp.bfloat16),
+            pltpu.VMEM((step * 2 * sides, table.shape[0]), jnp.bfloat16),
+        ],
+        compiler_params=pltpu.CompilerParams(vmem_limit_bytes=VMEM_LIMIT),
+        cost_estimate=pl.CostEstimate(
+            flops=25000000000, bytes_accessed=1000, transcendentals=0
+        ),
+        name="near_rest",
+    )(index, above, below, cells_above, cells_below, table, cells, u)
 
 
 def spread(table_ref, at, pair):
@@ -179,24 +233,27 @@
     return jnp.where(low, table_ref[first], table_ref[second])
 
 
-def parent_kernel(index_ref, pairs_ref, coupling_ref, transfer_ref, down_ref, table_ref, lhs_ref):
+def parent_kernel(pieces, index_ref, *rest):
+    pairs_refs = rest[:pieces]
+    coupling_ref, transfer_ref, down_ref, table_ref, lhs_ref = rest[pieces:]
     count, sides, _ = down_ref.shape
     slots = coupling_ref.shape[2] // 64
-    pairs = pairs_ref.shape[0]
+    pairs = pairs_refs[0].shape[0]
     low = low_lanes(sides)
     g = pl.program_id(0)
 
     @pl.when(g == 0)
     def _():
-        table_ref[2 * pairs] = jnp.zeros(table_ref.shape[1:], jnp.bfloat16)
-
-        def group(first, carry):
-            for extra in range(8):
-                at = first * 8 + extra
-                spread(table_ref, 2 * at, pairs_ref[at])
-            return carry
-
-        lax.fori_loop(0, pairs // 8, group, 0)
+        table_ref[2 * pieces * pairs] = jnp.zeros(table_ref.shape[1:], jnp.bfloat16)
+        for number, pairs_ref in enumerate(pairs_refs):
+
+            def group(first, carry):
+                for extra in range(8):
+                    at = first * 8 + extra
+                    spread(table_ref, 2 * (number * pairs + at), pairs_ref[at])
+                return carry
+
+            lax.fori_loop(0, pairs // 8, group, 0)
 
     for pair in range(count // 2):
         for half in range(2):
@@ -222,36 +279,38 @@
         down_ref[2 * pair + 1] = d[sides:]
 
 
-def parents_down(index, pairs, coupling, transfer):
+def parents_down(index, pieces, coupling, transfer):
     parents, _, width = coupling.shape
-    sides = pairs.shape[1]
+    pairs, sides, _ = pieces[0].shape
     step = 8
     return pl.pallas_call(
-        parent_kernel,
+        functools.partial(parent_kernel, len(pieces)),
         grid=(parents // step,),
         in_specs=[
             pl.BlockSpec(memory_space=pltpu.SMEM),
-            pl.BlockSpec(pairs.shape, lambda g: (0, 0, 0)),
+        ]
+        + [pl.BlockSpec(pieces[0].shape, lambda g: (0, 0, 0))] * len(pieces)
+        + [
             pl.BlockSpec((step, 64, width), lambda g: (g, 0, 0)),
             pl.BlockSpec((step, 64, 256), lambda g: (g, 0, 0)),
         ],
         out_specs=pl.BlockSpec((step, sides, 256), lambda g: (g, 0, 0)),
         out_shape=jax.ShapeDtypeStruct((parents, sides, 256), jnp.float32),
         scratch_shapes=[
-            pltpu.VMEM((2 * pairs.shape[0] + 1, sides, 128), jnp.bfloat16),
+            pltpu.VMEM((2 * len(pieces) * pairs + 1, sides, 128), jnp.bfloat16),
             pltpu.VMEM((2 * sides, (width + 127) // 128 * 128), jnp.bfloat16),
         ],
         compiler_params=pltpu.CompilerParams(vmem_limit_bytes=VMEM_LIMIT),
         cost_estimate=pl.CostEstimate(
-            flops=4_000_000_000, bytes_accessed=14_000_000, transcendentals=0
+            flops=17000000000, bytes_accessed=1000, transcendentals=0
         ),
         name="parents_down",
-    )(index, pairs, coupling, transfer)
+    )(index, *pieces, coupling, transfer)
 
 
 def final_kernel(pieces, index_ref, *rest):
     piece_refs = rest[:pieces]
-    coupling_ref, down_ref, basis_ref, cells_ref, u_ref, out_ref, table_ref, lhs_ref = rest[pieces:]
+    coupling_ref, down_ref, basis_ref, near_ref, out_ref, table_ref, lhs_ref = rest[pieces:]
     parents, sides, _ = down_ref.shape
     slots = coupling_ref.shape[2] // 64
     per_piece = piece_refs[0].shape[0]
@@ -296,15 +355,11 @@
         ).astype(jnp.bfloat16)
         far = dot(own, basis_ref[4 * p : 4 * p + 4].reshape(256, 128), NN)
         for c in range(4):
-            t = 4 * p + c
-            hot = one_hot(cells_ref[t : t + 1, :])
-            near = dot(jnp.concatenate(split(u_ref[t]), axis=0), hot, NN)
-            out_ref[:, t * 128 : (t + 1) * 128] = (
-                far[c * sides : (c + 1) * sides] + near[:sides] + near[sides:]
-            )
-
-
-def finish(index, pieces, coupling, down, basis, cells, u):
+            columns = slice((4 * p + c) * 128, (4 * p + c + 1) * 128)
+            out_ref[:, columns] = far[c * sides : (c + 1) * sides] + near_ref[:, columns]
+
+
+def finish(index, pieces, coupling, down, basis, near):
     leaves, _, width = coupling.shape
     sides = down.shape[1]
     step = 16
@@ -318,8 +373,7 @@
             pl.BlockSpec((step, 64, width), lambda g: (g, 0, 0)),
             pl.BlockSpec((step // 4, sides, 256), lambda g: (g, 0, 0)),
             pl.BlockSpec((step, 64, 128), lambda g: (g, 0, 0)),
-            pl.BlockSpec((step, 128), lambda g: (g, 0)),
-            pl.BlockSpec((step, sides, CELLS), lambda g: (g, 0, 0)),
+            pl.BlockSpec((sides, step * 128), lambda g: (0, g)),
         ],
         out_specs=pl.BlockSpec((sides, step * 128), lambda g: (0, g)),
         out_shape=jax.ShapeDtypeStruct((sides, leaves * 128), jnp.float32),
@@ -329,10 +383,30 @@
         ],
         compiler_params=pltpu.CompilerParams(vmem_limit_bytes=VMEM_LIMIT),
         cost_estimate=pl.CostEstimate(
-            flops=6_000_000_000, bytes_accessed=20_000_000, transcendentals=0
+            flops=18000000000, bytes_accessed=1000, transcendentals=0
         ),
         name="finish",
-    )(index, *pieces, coupling, down, basis, cells, u)
+    )(index, *pieces, coupling, down, basis, near)
+
+
+def gather_parents(pairs):
+    sibs, at = lax.axis_size("sib"), lax.axis_index("sib")
+    line = [pairs]
+    for shift in range(1, sibs):
+        turn = [(i, (i + shift) % sibs) for i in range(sibs)]
+        line.append(lax.ppermute(pairs, "sib", turn))
+    line = jnp.concatenate(line, axis=0)
+    every = lax.all_gather(line, "leaf", axis=0, tiled=True)
+    return [every], lambda leaf, sib: leaf * sibs + jnp.remainder(at - sib, sibs)
+
+
+def gather_leaves(block):
+    sibs, at = lax.axis_size("sib"), lax.axis_index("sib")
+    turns = [
+        lax.ppermute(block, "sib", [(i, (i + shift) % sibs) for i in range(sibs)])
+        for shift in range(1, sibs)
+    ]
+    return [block] + turns, lambda sib: jnp.remainder(at - sib, sibs)
 
 
 def body(
@@ -362,11 +436,7 @@
     after = lax.ppermute(packed, everyone, downward)
 
     leaf_coef, parent_pairs = coefficients(points_x, basis, transfer)
-    every_parent = lax.all_gather(parent_pairs, everyone, axis=0, tiled=True)
-    pieces = [leaf_coef]
-    for shift in range(1, sibs):
-        turn = [(i, (i + shift) % sibs) for i in range(sibs)]
-        pieces.append(lax.ppermute(leaf_coef, "sib", turn))
+    parent_pieces, parent_place = gather_parents(parent_pairs)
 
     own_cells = (coords[1] * 16 + coords[0]).reshape(leaves, leaf_size)
 
@@ -376,27 +446,43 @@
 
     leaf_ids = jnp.arange(leaves, dtype=jnp.int32)[:, None]
     steps = jnp.arange(3, dtype=jnp.int32)[None, :] - 1
-    near_index = jnp.where(
-        near_list.reshape(leaves, 3, 3) >= 0, (leaf_ids + steps)[:, None, :], leaves
+    own_list = near_list[:, 3:6]
+    own_index = jnp.where(own_list >= 0, leaf_ids + steps, leaves)
+    rest_list = jnp.concatenate([near_list[:, :3], near_list[:, 6:]], axis=1)
+    rest_place = jnp.concatenate([leaf_ids + steps, leaves + leaf_ids + steps], axis=1)
+    rest_index = jnp.where(rest_list >= 0, rest_place, 2 * leaves)
+
+    owner = parent_list // parents
+    parent_index = jnp.where(
+        parent_list >= 0,
+        parent_place(owner // sibs, owner % sibs) * parents + parent_list % parents,
+        devices * parents,
     )
 
-    def row_index(row):
-        return near_index[:, row].reshape(-1)
-
-    me = lax.axis_index("sib")
-    group_base = lax.axis_index("leaf") * (sibs * leaves)
-    local = leaf_list - group_base
-    piece = jnp.bitwise_and(me - local // leaves + sibs, sibs - 1)
-    leaf_index = jnp.where(leaf_list >= 0, piece * leaves + local % leaves, sibs * leaves)
-    parent_index = jnp.where(parent_list >= 0, parent_list, parents * devices)
-
-    u = near_row(row_index(1), points_x, own_cells, table[1])
-    u = near_row(row_index(0), before[:, : leaves * leaf_size], cells_of(before), table[0], u)
-    u = near_row(row_index(2), after[:, : leaves * leaf_size], cells_of(after), table[2], u)
-    down = parents_down(parent_index.reshape(-1), every_parent, parent_coupling, transfer)
-    return finish(
-        leaf_index.reshape(-1), pieces, leaf_coupling, down, basis, own_cells, u
+    def indices_of_leaves(leaf_place, leaf_pieces):
+        local = leaf_list - lax.axis_index("leaf") * (sibs * leaves)
+        return jnp.where(
+            leaf_list >= 0,
+            leaf_place(local // leaves) * leaves + local % leaves,
+            len(leaf_pieces) * leaves,
+        )
+
+    u = near_own(own_index.reshape(-1), points_x, own_cells, table[1])
+    leaf_coef, _ = lax.optimization_barrier((leaf_coef, (before, after)))
+    leaf_pieces, leaf_place = gather_leaves(leaf_coef)
+    leaf_index = indices_of_leaves(leaf_place, leaf_pieces)
+    near = near_rest(
+        rest_index.reshape(-1),
+        before,
+        after,
+        cells_of(before),
+        cells_of(after),
+        jnp.concatenate([table[0], table[2]], axis=0),
+        own_cells,
+        u,
     )
+    down = parents_down(parent_index.reshape(-1), parent_pieces, parent_coupling, transfer)
+    return finish(leaf_index.reshape(-1), leaf_pieces, leaf_coupling, down, basis, near)
 
 
 def solution(mesh):

time: 174 us -> 148 us (0.85)
  waiting for transfers between devices: 53.9 us -> 32.8 us
  Pallas kernels: 79.6 us -> 73.2 us
  starting transfers between devices: 12.8 us -> 17.6 us
  local copies, waits for them, and re-layouts: 11.1 us -> 6.35 us
  other arithmetic: 1.57 us -> 3.51 us
    all_gather x1, waiting for transfers between devices: 23.8 us -> 0.01 us  [gather_parents(): every = lax.all_gather(line, 'leaf', axis=0, tiled=True)]
    ppermute x3 -> x6, starting transfers between devices: 6.52 us -> 12.7 us  [the longest x3 7 us: gather_parents(): line.append(lax.ppermute(pairs, 'sib', turn))]
    pallas_call x4 -> x3, Pallas kernels: 56.3 us -> 51.5 us  [the longest x1 23 us: near_rest(): pl.pallas_call(near_rest_kernel, grid=(leaves // step,), in_specs=[pl.Blo...]
    ppermute x1, waiting for transfers between devices: 0.01 us -> 4.59 us  [body(): before = lax.ppermute(packed, everyone, upward)]
    ppermute x1, waiting for transfers between devices: 30.1 us -> 25.7 us  [body(): after = lax.ppermute(packed, everyone, downward)]
    another operation x3 -> x0, local copies, waits for them, and re-layouts: 3.97 us -> none  [row_index(): return near_index[:, row].reshape(-1)]
    slice x3 -> x0, local copies, waits for them, and re-layouts: 2.81 us -> none  [the longest x1 1.13 us: body(): before[:, :leaves * leaf_size]]
    ppermute x3 -> x6, waiting for transfers between devices: 0.01 us -> 2.42 us  [the longest x3 2.41 us: gather_parents(): line.append(lax.ppermute(pairs, 'sib', turn))]
  transfers between devices with their start and end apart: 6 -> 9, of which waited for: 2 -> 3; matrix products, arithmetic and copies ran while one was open for 7% -> 5% of each run, Pallas kernels for 36% -> 35%
where the time goes in v2:
time: 148 us; the launch traced here: 147 us
  Pallas kernels  73.2 us (49%)
  waiting for transfers between devices  32.8 us (22%)
  starting transfers between devices  17.6 us (12%)
  between operations  13.5 us (9%)
  local copies, waits for them, and re-layouts  6.35 us (4%)
  other arithmetic  3.51 us (2%)
    ppermute x1, waiting for transfers between devices, body(): after = lax.ppermute(packed, everyone, downward)  25.7 us
    pallas_call x1, Pallas kernels, near_rest(): pl.pallas_call(near_rest_kernel, grid=(leaves // step,), in_specs=[pl.Blo...  23 us
    pallas_call x1, Pallas kernels, finish(): pl.pallas_call(functools.partial(final_kernel, len(pieces)), grid=(leaves...  16.1 us
    pallas_call x1, Pallas kernels, parents_down(): pl.pallas_call(functools.partial(parent_kernel, len(pieces)), grid=(paren...  16 us
    pallas_call x1, Pallas kernels, near_own(): pl.pallas_call(near_own_kernel, grid=(leaves // step,), in_specs=[pl.Bloc...  12.5 us
    ppermute x3, starting transfers between devices, gather_parents(): line.append(lax.ppermute(pairs, 'sib', turn))  7 us
    ppermute x3, starting transfers between devices, gather_leaves(): lax.ppermute(block, 'sib', [(i, (i + shift) % sibs) for i in range(sibs)])  5.74 us
    pallas_call x1, Pallas kernels, coefficients(): pl.pallas_call(coef_kernel, grid=(parents // step,), in_specs=[pl.BlockSp...  5.59 us
  transfers between devices with their start and end apart: 9, of which 3 were waited for; matrix products, arithmetic and copies ran while one was open for 5% of the time, Pallas kernels for 35%

profile of v2, /device:TPU:0, one launch (start us, length us, event | category | flops | bytes accessed | tf_op | source)
XLA Modules:
  0.0 147.0 jit_solution(15894264749581465629)
XLA Ops:
  6.5 0.0 copy-start
  6.5 0.0 all-gather.2.cloned.1.call-start
  6.5 5.6 %coefficients.1 = (bf16[32,32,256]{2,1,0:T(8,128)(2,1)}, bf16[16,32,128]{2,1,0:T(8,128)(2,1)}) custom-call(bf16[32,16384]{1,0:T(8,128)(2,1)} %x_ref.3, bf16[128,64,128]{2,1,0:T(8,128)(2,1)} %rest_6_.1, bf16[32,64,256]{2,1,0:T(8,128)(2,1)} %rest_2_.1), custom_call_target="tpu_custom_call" | custom-call | flops 1000000 | bytes 1000 | tf_op jit(solution)/shard_map/coefficients/pallas_call | solution.py:81
  12.1 0.0 copy-start.1
  12.1 0.0 copy-start.2
  12.1 3.1 %collective-permute-start.5 = (bf16[16,32,128]{2,1,0:T(8,128)(2,1)}, bf16[16,32,128]{2,1,0:T(8,128)(2,1)S(1)}, u32[]{:S(2)}, u32[]{:S(2)}) collective-permute-start(bf16[16,32,128]{2,1,0:T(8,128)(2,1)} %get-tuple-element.10), channel_id=1, source_target_pairs={{0,1},{1,2},{2,3},{3,0},{4,5},{5,6},{6,7},{7,4},{8,9},{9,10},{10,1... | collective-permute-start | bytes 393224 | tf_op jit(solution)/shard_map/ppermute | solution.py:397
  15.2 2.6 %collective-permute-start.6 = (bf16[16,32,128]{2,1,0:T(8,128)(2,1)}, bf16[16,32,128]{2,1,0:T(8,128)(2,1)S(1)}, u32[]{:S(2)}, u32[]{:S(2)}) collective-permute-start(bf16[16,32,128]{2,1,0:T(8,128)(2,1)} %get-tuple-element.10), channel_id=1, source_target_pairs={{0,2},{1,3},{2,0},{3,1},{4,6},{5,7},{6,4},{7,5},{8,10},{9,11},{10,... | collective-permute-start | bytes 393224 | tf_op jit(solution)/shard_map/ppermute | solution.py:397
  17.8 1.3 collective-permute-start.7
  19.1 0.0 copy-done
  19.1 0.1 constant_dynamic-update-slice_fusion.1
  19.2 0.0 copy-done.1
  19.2 0.0 copy-start.4
  19.3 0.0 copy-start.3
  19.4 0.0 copy-start.5
  19.4 3.6 %collective-permute-start = (bf16[32,17408]{1,0:T(8,128)(2,1)S(1)}, bf16[32,17408]{1,0:T(8,128)(2,1)}, u32[]{:S(2)}, u32[]{:S(2)}) collective-permute-start(bf16[32,17408]{1,0:T(8,128)(2,1)S(1)} %constant_dynamic-update-slice_fusion), channel_id=1, source_target_pairs={{0,1},{1,2},{2,3},{3,4},{4,5},{5,6},{6,7},{7,8},{8,9},{9,10},{10,1... | collective-permute-start | bytes 3342344 | tf_op jit(solution)/shard_map/ppermute | solution.py:435
  23.0 1.3 collective-permute-start.1
  24.3 0.0 collective-permute-done.5
  24.3 2.4 %collective-permute-done.6 = bf16[16,32,128]{2,1,0:T(8,128)(2,1)S(1)} collective-permute-done((bf16[16,32,128]{2,1,0:T(8,128)(2,1)}, bf16[16,32,128]{2,1,0:T(8,128)(2,1)S(1)}, u32[]{:S(2)}, u32[]{:S(2)}) %collective-permute-start.6) | collective-permute-done | bytes 131104 | tf_op jit(solution)/shard_map/ppermute | solution.py:397
  26.7 0.0 collective-permute-done.7
  26.7 0.0 copy-done.2
  26.7 0.9 pad_maximum_fusion
  27.5 0.0 all-gather.2.cloned.1.call-update
  27.6 0.7 slice_add_fusion.2
  28.3 0.0 copy-done.4
  28.3 0.1 fusion.16
  28.4 0.1 copy.15
  28.5 0.7 select_n.69.index_ref
  29.2 0.1 copy.16
  29.3 0.7 reshape.54.index_ref
  30.1 0.0 copy-done.3
  30.1 0.7 reshape.53.index_ref
  30.8 0.0 copy-done.5
  30.9 0.1 copy.14
  31.0 0.7 reshape.51.index_ref
  31.6 0.0 copy-start.6
  31.6 12.5 %near_own.1.u_ref = f32[128,32,256]{2,1,0:T(8,128)} custom-call(s32[384]{0:T(512)} %reshape.54.index_ref, bf16[32,16384]{1,0:T(8,128)(2,1)} %x_ref.3, s32[128,128]{1,0:T(8,128)} %bitcast.1, bf16[768,256]{1,0:T(8,128)(2,1)} %constant.120.table_ref), custom_call_target="tpu_custom_call" | custom-call | flops 1000000 | bytes 1000 | tf_op jit(solution)/shard_map/near_own/pallas_call | solution.py:148
  44.1 4.6 %collective-permute-done.above_ref = bf16[32,17408]{1,0:T(8,128)(2,1)} collective-permute-done((bf16[32,17408]{1,0:T(8,128)(2,1)S(1)}, bf16[32,17408]{1,0:T(8,128)(2,1)}, u32[]{:S(2)}, u32[]{:S(2)}) %collective-permute-start) | collective-permute-done | bytes 1114144 | tf_op jit(solution)/shard_map/ppermute | solution.py:435
  48.7 25.7 %collective-permute-done.1.below_ref = bf16[32,17408]{1,0:T(8,128)(2,1)} collective-permute-done((bf16[32,17408]{1,0:T(8,128)(2,1)S(1)}, bf16[32,17408]{1,0:T(8,128)(2,1)}, u32[]{:S(2)}, u32[]{:S(2)}) %collective-permute-start.1) | collective-permute-done | bytes 1114144 | tf_op jit(solution)/shard_map/ppermute | solution.py:436
  74.4 0.0 copy-done.6
  74.4 3.4 %collective-permute-start.2 = (bf16[32,32,256]{2,1,0:T(8,128)(2,1)S(1)}, bf16[32,32,256]{2,1,0:T(8,128)(2,1)S(1)}, u32[]{:S(2)}, u32[]{:S(2)}) collective-permute-start(bf16[32,32,256]{2,1,0:T(8,128)(2,1)S(1)} %copy-done.6), channel_id=1, source_target_pairs={{0,1},{1,2},{2,3},{3,0},{4,5},{5,6},{6,7},{7,4},{8,9},{9,10},{10,1... | collective-permute-start | bytes 1572872 | tf_op jit(solution)/shard_map/ppermute | solution.py:406
  77.8 0.0 collective-permute-start.3
  77.8 2.4 %collective-permute-start.4 = (bf16[32,32,256]{2,1,0:T(8,128)(2,1)S(1)}, bf16[32,32,256]{2,1,0:T(8,128)(2,1)S(1)}, u32[]{:S(2)}, u32[]{:S(2)}) collective-permute-start(bf16[32,32,256]{2,1,0:T(8,128)(2,1)S(1)} %copy-done.6), channel_id=1, source_target_pairs={{0,3},{1,0},{2,1},{3,2},{4,7},{5,4},{6,5},{7,6},{8,11},{9,8},{10,9... | collective-permute-start | bytes 1572872 | tf_op jit(solution)/shard_map/ppermute | solution.py:406
  80.2 0.9 slice_convert_fusion.1
  81.0 0.6 add.125.cells_above_ref
  81.7 0.9 slice_convert_fusion
  82.5 0.6 add.127.cells_below_ref
  83.2 23.0 %near_rest.1.rest_7_ = f32[32,16384]{1,0:T(8,128)} custom-call(s32[768]{0:T(1024)} %select_n.69.index_ref, bf16[32,17408]{1,0:T(8,128)(2,1)} %collective-permute-done.above_ref, bf16[32,17408]{1,0:T(8,128)(2,1)} %collective-permute-done.1.below_ref, s32[128,128]{1,0:T(8,128)} %add.125.cells_above_ref, s32[128,128]{1,0:T(8,128)} %add.127.cells_below_ref, ...), custom_call_target="tpu_custom_call" | custom-call | flops 24999999488 | bytes 1000 | tf_op jit(solution)/shard_map/near_rest/pallas_call | solution.py:196
  106.2 0.0 all-gather.2.cloned.1.call-done.rest_0_
  106.2 16.0 %parents_down.1.rest_5_ = f32[32,32,256]{2,1,0:T(8,128)} custom-call(s32[864]{0:T(1024)} %reshape.53.index_ref, bf16[512,32,128]{2,1,0:T(8,128)(2,1)} %all-gather.2.cloned.1.call-done.rest_0_, bf16[32,64,1728]{2,1,0:T(8,128)(2,1)} %rest_1_.1, bf16[32,64,256]{2,1,0:T(8,128)(2,1)} %rest_2_.1), custom_call_target="tpu_custom_call" | custom-call | flops 16999999488 | bytes 1000 | tf_op jit(solution)/shard_map/parents_down/pallas_call | solution.py:286
  122.2 0.0 collective-permute-done.2.rest_1_
  122.2 0.0 copy-start.7
  122.2 0.0 collective-permute-done.3.rest_2_
  122.2 0.0 copy-start.8
  122.2 0.0 collective-permute-done.4.rest_3_
  122.3 0.8 copy-done.7
  123.0 0.2 copy-done.8
  123.2 0.0 copy-start.9
  123.2 0.8 copy-done.9
  124.0 16.1 %finish.1 = f32[32,16384]{1,0:T(8,128)} custom-call(s32[1024]{0:T(1024)} %reshape.51.index_ref, bf16[32,32,256]{2,1,0:T(8,128)(2,1)} %get-tuple-element.9.rest_0_, bf16[32,32,256]{2,1,0:T(8,128)(2,1)} %copy-done.7, bf16[32,32,256]{2,1,0:T(8,128)(2,1)} %copy-done.8, bf16[32,32,256]{2,1,0:T(8,128)(2,1)} %copy-done.9, bf16[128,64,512]{2,1,0:T(8,128)(2,1)} %rest_4_.1, ...), custom_call_target="tpu_custom_call" | custom-call | flops 17999998976 | bytes 1000 | tf_op jit(solution)/shard_map/finish/pallas_call | solution.py:367
  (10 shorter events, 0.2 us)
Async XLA Ops:
  6.5 12.6 %copy-start = (bf16[32,16384]{1,0:T(8,128)(2,1)S(1)}, bf16[32,16384]{1,0:T(8,128)(2,1)}, u32[]{:S(2)}) copy-start(bf16[32,16384]{1,0:T(8,128)(2,1)} %x_ref.3) | copy-start | bytes 3145732
  6.5 99.6 %all-gather.2.cloned.1.call-start = ((), (), s32[]{:S(2)}) async-start(), calls=%async_computation | async-start | bytes 4718592 | tf_op jit(solution)/shard_map/all_gather | solution.py:399
  12.1 7.1 %copy-start.1 = (s32[2,16384]{1,0:T(2,128)S(1)}, s32[2,16384]{1,0:T(2,128)}, u32[]{:S(2)}) copy-start(s32[2,16384]{1,0:T(2,128)} %param.11) | copy-start | bytes 393220
  12.1 14.5 %copy-start.2 = (bf16[16,32,128]{2,1,0:T(8,128)(2,1)S(1)}, bf16[16,32,128]{2,1,0:T(8,128)(2,1)}, u32[]{:S(2)}) copy-start(bf16[16,32,128]{2,1,0:T(8,128)(2,1)} %get-tuple-element.10) | copy-start | bytes 393220
  12.1 12.1 %collective-permute-start.5 = (bf16[16,32,128]{2,1,0:T(8,128)(2,1)}, bf16[16,32,128]{2,1,0:T(8,128)(2,1)S(1)}, u32[]{:S(2)}, u32[]{:S(2)}) collective-permute-start(bf16[16,32,128]{2,1,0:T(8,128)(2,1)} %get-tuple-element.10), channel_id=1, source_target_pairs={{0,1},{1,2},{2,3},{3,0},{4,5},{5,6},{6,7},{7,4},{8,9},{9,10},{10,1... | collective-permute-start | bytes 393224 | tf_op jit(solution)/shard_map/ppermute | solution.py:397
  15.2 11.5 %collective-permute-start.6 = (bf16[16,32,128]{2,1,0:T(8,128)(2,1)}, bf16[16,32,128]{2,1,0:T(8,128)(2,1)S(1)}, u32[]{:S(2)}, u32[]{:S(2)}) collective-permute-start(bf16[16,32,128]{2,1,0:T(8,128)(2,1)} %get-tuple-element.10), channel_id=1, source_target_pairs={{0,2},{1,3},{2,0},{3,1},{4,6},{5,7},{6,4},{7,5},{8,10},{9,11},{10,... | collective-permute-start | bytes 393224 | tf_op jit(solution)/shard_map/ppermute | solution.py:397
  17.8 8.9 %collective-permute-start.7 = (bf16[16,32,128]{2,1,0:T(8,128)(2,1)}, bf16[16,32,128]{2,1,0:T(8,128)(2,1)S(1)}, u32[]{:S(2)}, u32[]{:S(2)}) collective-permute-start(bf16[16,32,128]{2,1,0:T(8,128)(2,1)} %get-tuple-element.10), channel_id=1, source_target_pairs={{0,3},{1,0},{2,1},{3,2},{4,7},{5,4},{6,5},{7,6},{8,11},{9,8},{10,9... | collective-permute-start | bytes 393224 | tf_op jit(solution)/shard_map/ppermute | solution.py:397
  19.2 9.1 %copy-start.4 = (s32[128,9]{0,1:T(8,128)S(1)}, s32[128,9]{0,1:T(8,128)}, u32[]{:S(2)}) copy-start(s32[128,9]{0,1:T(8,128)} %param.12) | copy-start | bytes 13828
  19.3 10.7 %copy-start.3 = (s32[32,27]{1,0:T(8,128)S(1)}, s32[32,27]{1,0:T(8,128)}, u32[]{:S(2)}) copy-start(s32[32,27]{1,0:T(8,128)} %param.14) | copy-start | bytes 10372
  19.4 11.5 %copy-start.5 = (s32[128,8]{0,1:T(8,128)S(1)}, s32[128,8]{0,1:T(8,128)}, u32[]{:S(2)}) copy-start(s32[128,8]{0,1:T(8,128)} %param.13) | copy-start | bytes 12292
  19.4 29.3 %collective-permute-start = (bf16[32,17408]{1,0:T(8,128)(2,1)S(1)}, bf16[32,17408]{1,0:T(8,128)(2,1)}, u32[]{:S(2)}, u32[]{:S(2)}) collective-permute-start(bf16[32,17408]{1,0:T(8,128)(2,1)S(1)} %constant_dynamic-update-slice_fusion), channel_id=1, source_target_pairs={{0,1},{1,2},{2,3},{3,4},{4,5},{5,6},{6,7},{7,8},{8,9},{9,10},{10,1... | collective-permute-start | bytes 3342344 | tf_op jit(solution)/shard_map/ppermute | solution.py:435
  23.0 51.4 %collective-permute-start.1 = (bf16[32,17408]{1,0:T(8,128)(2,1)S(1)}, bf16[32,17408]{1,0:T(8,128)(2,1)}, u32[]{:S(2)}, u32[]{:S(2)}) collective-permute-start(bf16[32,17408]{1,0:T(8,128)(2,1)S(1)} %constant_dynamic-update-slice_fusion), channel_id=1, source_target_pairs={{1,0},{2,1},{3,2},{4,3},{5,4},{6,5},{7,6},{8,7},{9,8},{10,9},{11,1... | collective-permute-start | bytes 3342344 | tf_op jit(solution)/shard_map/ppermute | solution.py:436
  31.6 42.8 %copy-start.6 = (bf16[32,32,256]{2,1,0:T(8,128)(2,1)S(1)}, bf16[32,32,256]{2,1,0:T(8,128)(2,1)}, u32[]{:S(2)}) copy-start(bf16[32,32,256]{2,1,0:T(8,128)(2,1)} %get-tuple-element.9.rest_0_) | copy-start | bytes 1572868
  74.4 47.8 %collective-permute-start.2 = (bf16[32,32,256]{2,1,0:T(8,128)(2,1)S(1)}, bf16[32,32,256]{2,1,0:T(8,128)(2,1)S(1)}, u32[]{:S(2)}, u32[]{:S(2)}) collective-permute-start(bf16[32,32,256]{2,1,0:T(8,128)(2,1)S(1)} %copy-done.6), channel_id=1, source_target_pairs={{0,1},{1,2},{2,3},{3,0},{4,5},{5,6},{6,7},{7,4},{8,9},{9,10},{10,1... | collective-permute-start | bytes 1572872 | tf_op jit(solution)/shard_map/ppermute | solution.py:406
  77.8 44.4 %collective-permute-start.3 = (bf16[32,32,256]{2,1,0:T(8,128)(2,1)S(1)}, bf16[32,32,256]{2,1,0:T(8,128)(2,1)S(1)}, u32[]{:S(2)}, u32[]{:S(2)}) collective-permute-start(bf16[32,32,256]{2,1,0:T(8,128)(2,1)S(1)} %copy-done.6), channel_id=1, source_target_pairs={{0,2},{1,3},{2,0},{3,1},{4,6},{5,7},{6,4},{7,5},{8,10},{9,11},{10,... | collective-permute-start | bytes 1572872 | tf_op jit(solution)/shard_map/ppermute | solution.py:406
  77.8 44.5 %collective-permute-start.4 = (bf16[32,32,256]{2,1,0:T(8,128)(2,1)S(1)}, bf16[32,32,256]{2,1,0:T(8,128)(2,1)S(1)}, u32[]{:S(2)}, u32[]{:S(2)}) collective-permute-start(bf16[32,32,256]{2,1,0:T(8,128)(2,1)S(1)} %copy-done.6), channel_id=1, source_target_pairs={{0,3},{1,0},{2,1},{3,2},{4,7},{5,4},{6,5},{7,6},{8,11},{9,8},{10,9... | collective-permute-start | bytes 1572872 | tf_op jit(solution)/shard_map/ppermute | solution.py:406
  122.2 0.8 copy-start.7
  122.2 1.0 copy-start.8
  123.2 0.8 copy-start.9
Sparse Core Ops, SparseCore 0:
  27.7 66.8 all-gather.1

commit v3 on v2

--- a/solution.py
+++ b/solution.py
@@ -144,7 +144,7 @@
 
 def near_own(index, x, cells, table):
     sides, leaves = x.shape[0], cells.shape[0]
-    step = 16
+    step = 32
     return pl.pallas_call(
         near_own_kernel,
         grid=(leaves // step,),
@@ -190,7 +190,7 @@
 
 def near_rest(index, above, below, cells_above, cells_below, table, cells, u):
     leaves, sides, _ = u.shape
-    step = 16
+    step = 32
     row = pl.BlockSpec((sides, leaves * 128), lambda g: (0, 0))
     row_cells = pl.BlockSpec((leaves, 128), lambda g: (0, 0))
     return pl.pallas_call(
@@ -362,7 +362,7 @@
 def finish(index, pieces, coupling, down, basis, near):
     leaves, _, width = coupling.shape
     sides = down.shape[1]
-    step = 16
+    step = 32
     whole = pl.BlockSpec(pieces[0].shape, lambda g: (0, 0, 0))
     return pl.pallas_call(
         functools.partial(final_kernel, len(pieces)),

time: 148 us -> 145 us (0.980)
  Pallas kernels: 73.2 us -> 70.2 us
  transfers between devices with their start and end apart: 9 -> 9, of which waited for: 3 -> 3; matrix products, arithmetic and copies ran while one was open for 5% -> 6% of each run, Pallas kernels for 35% -> 34%
where the time goes in v3:
time: 145 us
  Pallas kernels  70.2 us (48%)
  waiting for transfers between devices  33.7 us (23%)
  starting transfers between devices  17.6 us (12%)
  between operations  13.5 us (9%)
  local copies, waits for them, and re-layouts  6.35 us (4%)
  other arithmetic  3.51 us (2%)
    ppermute x1, waiting for transfers between devices, body(): after = lax.ppermute(packed, everyone, downward)  25.7 us
    pallas_call x1, Pallas kernels, near_rest(): pl.pallas_call(near_rest_kernel, grid=(leaves // step,), in_specs=[pl.Blo...  21.8 us
    pallas_call x1, Pallas kernels, parents_down(): pl.pallas_call(functools.partial(parent_kernel, len(pieces)), grid=(paren...  16 us
    pallas_call x1, Pallas kernels, finish(): pl.pallas_call(functools.partial(final_kernel, len(pieces)), grid=(leaves...  15.3 us
    pallas_call x1, Pallas kernels, near_own(): pl.pallas_call(near_own_kernel, grid=(leaves // step,), in_specs=[pl.Bloc...  11.5 us
    ppermute x3, starting transfers between devices, gather_parents(): line.append(lax.ppermute(pairs, 'sib', turn))  7 us
    ppermute x3, starting transfers between devices, gather_leaves(): lax.ppermute(block, 'sib', [(i, (i + shift) % sibs) for i in range(sibs)])  5.74 us
    pallas_call x1, Pallas kernels, coefficients(): pl.pallas_call(coef_kernel, grid=(parents // step,), in_specs=[pl.BlockSp...  5.59 us
  transfers between devices with their start and end apart: 9, of which 3 were waited for; matrix products, arithmetic and copies ran while one was open for 6% of the time, Pallas kernels for 34%

profile of v3, /device:TPU:0, one launch (start us, length us, event | category | flops | bytes accessed | tf_op | source)
XLA Modules:
  0.0 145.0 jit_solution(14931341850267512959)
XLA Ops:
  6.5 0.0 copy-start
  6.5 0.0 all-gather.2.cloned.1.call-start
  6.5 5.6 %coefficients.1 = (bf16[32,32,256]{2,1,0:T(8,128)(2,1)}, bf16[16,32,128]{2,1,0:T(8,128)(2,1)}) custom-call(bf16[32,16384]{1,0:T(8,128)(2,1)} %x_ref.3, bf16[128,64,128]{2,1,0:T(8,128)(2,1)} %rest_6_.1, bf16[32,64,256]{2,1,0:T(8,128)(2,1)} %rest_2_.1), custom_call_target="tpu_custom_call" | custom-call | flops 1000000 | bytes 1000 | tf_op jit(solution)/shard_map/coefficients/pallas_call | solution.py:81
  12.1 0.0 copy-start.1
  12.1 0.0 copy-start.2
  12.1 3.1 %collective-permute-start.5 = (bf16[16,32,128]{2,1,0:T(8,128)(2,1)}, bf16[16,32,128]{2,1,0:T(8,128)(2,1)S(1)}, u32[]{:S(2)}, u32[]{:S(2)}) collective-permute-start(bf16[16,32,128]{2,1,0:T(8,128)(2,1)} %get-tuple-element.10), channel_id=1, source_target_pairs={{0,1},{1,2},{2,3},{3,0},{4,5},{5,6},{6,7},{7,4},{8,9},{9,10},{10,1... | collective-permute-start | bytes 393224 | tf_op jit(solution)/shard_map/ppermute | solution.py:397
  15.2 2.6 %collective-permute-start.6 = (bf16[16,32,128]{2,1,0:T(8,128)(2,1)}, bf16[16,32,128]{2,1,0:T(8,128)(2,1)S(1)}, u32[]{:S(2)}, u32[]{:S(2)}) collective-permute-start(bf16[16,32,128]{2,1,0:T(8,128)(2,1)} %get-tuple-element.10), channel_id=1, source_target_pairs={{0,2},{1,3},{2,0},{3,1},{4,6},{5,7},{6,4},{7,5},{8,10},{9,11},{10,... | collective-permute-start | bytes 393224 | tf_op jit(solution)/shard_map/ppermute | solution.py:397
  17.8 1.3 collective-permute-start.7
  19.1 0.0 copy-done
  19.1 0.1 constant_dynamic-update-slice_fusion.1
  19.2 0.0 copy-done.1
  19.2 0.0 copy-start.4
  19.3 0.0 copy-start.3
  19.4 0.0 copy-start.5
  19.4 3.6 %collective-permute-start = (bf16[32,17408]{1,0:T(8,128)(2,1)S(1)}, bf16[32,17408]{1,0:T(8,128)(2,1)}, u32[]{:S(2)}, u32[]{:S(2)}) collective-permute-start(bf16[32,17408]{1,0:T(8,128)(2,1)S(1)} %constant_dynamic-update-slice_fusion), channel_id=1, source_target_pairs={{0,1},{1,2},{2,3},{3,4},{4,5},{5,6},{6,7},{7,8},{8,9},{9,10},{10,1... | collective-permute-start | bytes 3342344 | tf_op jit(solution)/shard_map/ppermute | solution.py:435
  23.0 1.3 collective-permute-start.1
  24.3 0.0 collective-permute-done.5
  24.3 2.4 %collective-permute-done.6 = bf16[16,32,128]{2,1,0:T(8,128)(2,1)S(1)} collective-permute-done((bf16[16,32,128]{2,1,0:T(8,128)(2,1)}, bf16[16,32,128]{2,1,0:T(8,128)(2,1)S(1)}, u32[]{:S(2)}, u32[]{:S(2)}) %collective-permute-start.6) | collective-permute-done | bytes 131104 | tf_op jit(solution)/shard_map/ppermute | solution.py:397
  26.7 0.0 collective-permute-done.7
  26.7 0.0 copy-done.2
  26.7 0.9 pad_maximum_fusion
  27.5 0.0 all-gather.2.cloned.1.call-update
  27.6 0.7 slice_add_fusion.2
  28.3 0.0 copy-done.4
  28.3 0.1 fusion.16
  28.4 0.1 copy.15
  28.5 0.7 select_n.69.index_ref
  29.2 0.1 copy.16
  29.3 0.7 reshape.54.index_ref
  30.1 0.0 copy-done.3
  30.1 0.7 reshape.53.index_ref
  30.8 0.0 copy-done.5
  30.9 0.1 copy.14
  31.0 0.7 reshape.51.index_ref
  31.6 0.0 copy-start.6
  31.6 11.5 %near_own.1.u_ref = f32[128,32,256]{2,1,0:T(8,128)} custom-call(s32[384]{0:T(512)} %reshape.54.index_ref, bf16[32,16384]{1,0:T(8,128)(2,1)} %x_ref.3, s32[128,128]{1,0:T(8,128)} %bitcast.1, bf16[768,256]{1,0:T(8,128)(2,1)} %constant.120.table_ref), custom_call_target="tpu_custom_call" | custom-call | flops 1000000 | bytes 1000 | tf_op jit(solution)/shard_map/near_own/pallas_call | solution.py:148
  43.1 5.6 %collective-permute-done.above_ref = bf16[32,17408]{1,0:T(8,128)(2,1)} collective-permute-done((bf16[32,17408]{1,0:T(8,128)(2,1)S(1)}, bf16[32,17408]{1,0:T(8,128)(2,1)}, u32[]{:S(2)}, u32[]{:S(2)}) %collective-permute-start) | collective-permute-done | bytes 1114144 | tf_op jit(solution)/shard_map/ppermute | solution.py:435
  48.7 25.7 %collective-permute-done.1.below_ref = bf16[32,17408]{1,0:T(8,128)(2,1)} collective-permute-done((bf16[32,17408]{1,0:T(8,128)(2,1)S(1)}, bf16[32,17408]{1,0:T(8,128)(2,1)}, u32[]{:S(2)}, u32[]{:S(2)}) %collective-permute-start.1) | collective-permute-done | bytes 1114144 | tf_op jit(solution)/shard_map/ppermute | solution.py:436
  74.4 0.0 copy-done.6
  74.4 3.4 %collective-permute-start.2 = (bf16[32,32,256]{2,1,0:T(8,128)(2,1)S(1)}, bf16[32,32,256]{2,1,0:T(8,128)(2,1)S(1)}, u32[]{:S(2)}, u32[]{:S(2)}) collective-permute-start(bf16[32,32,256]{2,1,0:T(8,128)(2,1)S(1)} %copy-done.6), channel_id=1, source_target_pairs={{0,1},{1,2},{2,3},{3,0},{4,5},{5,6},{6,7},{7,4},{8,9},{9,10},{10,1... | collective-permute-start | bytes 1572872 | tf_op jit(solution)/shard_map/ppermute | solution.py:406
  77.8 0.0 collective-permute-start.3
  77.8 2.4 %collective-permute-start.4 = (bf16[32,32,256]{2,1,0:T(8,128)(2,1)S(1)}, bf16[32,32,256]{2,1,0:T(8,128)(2,1)S(1)}, u32[]{:S(2)}, u32[]{:S(2)}) collective-permute-start(bf16[32,32,256]{2,1,0:T(8,128)(2,1)S(1)} %copy-done.6), channel_id=1, source_target_pairs={{0,3},{1,0},{2,1},{3,2},{4,7},{5,4},{6,5},{7,6},{8,11},{9,8},{10,9... | collective-permute-start | bytes 1572872 | tf_op jit(solution)/shard_map/ppermute | solution.py:406
  80.2 0.9 slice_convert_fusion.1
  81.0 0.6 add.125.cells_above_ref
  81.7 0.9 slice_convert_fusion
  82.5 0.6 add.127.cells_below_ref
  83.2 21.8 %near_rest.1.rest_7_ = f32[32,16384]{1,0:T(8,128)} custom-call(s32[768]{0:T(1024)} %select_n.69.index_ref, bf16[32,17408]{1,0:T(8,128)(2,1)} %collective-permute-done.above_ref, bf16[32,17408]{1,0:T(8,128)(2,1)} %collective-permute-done.1.below_ref, s32[128,128]{1,0:T(8,128)} %add.125.cells_above_ref, s32[128,128]{1,0:T(8,128)} %add.127.cells_below_ref, ...), custom_call_target="tpu_custom_call" | custom-call | flops 24999999488 | bytes 1000 | tf_op jit(solution)/shard_map/near_rest/pallas_call | solution.py:196
  105.0 0.0 all-gather.2.cloned.1.call-done.rest_0_
  105.0 16.0 %parents_down.1.rest_5_ = f32[32,32,256]{2,1,0:T(8,128)} custom-call(s32[864]{0:T(1024)} %reshape.53.index_ref, bf16[512,32,128]{2,1,0:T(8,128)(2,1)} %all-gather.2.cloned.1.call-done.rest_0_, bf16[32,64,1728]{2,1,0:T(8,128)(2,1)} %rest_1_.1, bf16[32,64,256]{2,1,0:T(8,128)(2,1)} %rest_2_.1), custom_call_target="tpu_custom_call" | custom-call | flops 16999999488 | bytes 1000 | tf_op jit(solution)/shard_map/parents_down/pallas_call | solution.py:286
  121.1 0.0 collective-permute-done.2.rest_1_
  121.1 0.0 copy-start.7
  121.1 0.0 collective-permute-done.3.rest_2_
  121.1 0.0 copy-start.8
  121.1 0.0 collective-permute-done.4.rest_3_
  121.1 0.8 copy-done.7
  121.9 0.2 copy-done.8
  122.0 0.0 copy-start.9
  122.0 0.8 copy-done.9
  122.8 15.3 %finish.1 = f32[32,16384]{1,0:T(8,128)} custom-call(s32[1024]{0:T(1024)} %reshape.51.index_ref, bf16[32,32,256]{2,1,0:T(8,128)(2,1)} %get-tuple-element.9.rest_0_, bf16[32,32,256]{2,1,0:T(8,128)(2,1)} %copy-done.7, bf16[32,32,256]{2,1,0:T(8,128)(2,1)} %copy-done.8, bf16[32,32,256]{2,1,0:T(8,128)(2,1)} %copy-done.9, bf16[128,64,512]{2,1,0:T(8,128)(2,1)} %rest_4_.1, ...), custom_call_target="tpu_custom_call" | custom-call | flops 17999998976 | bytes 1000 | tf_op jit(solution)/shard_map/finish/pallas_call | solution.py:367
  (10 shorter events, 0.2 us)
Async XLA Ops:
  6.5 12.6 %copy-start = (bf16[32,16384]{1,0:T(8,128)(2,1)S(1)}, bf16[32,16384]{1,0:T(8,128)(2,1)}, u32[]{:S(2)}) copy-start(bf16[32,16384]{1,0:T(8,128)(2,1)} %x_ref.3) | copy-start | bytes 3145732
  6.5 98.5 %all-gather.2.cloned.1.call-start = ((), (), s32[]{:S(2)}) async-start(), calls=%async_computation | async-start | bytes 4718592 | tf_op jit(solution)/shard_map/all_gather | solution.py:399
  12.1 7.1 %copy-start.1 = (s32[2,16384]{1,0:T(2,128)S(1)}, s32[2,16384]{1,0:T(2,128)}, u32[]{:S(2)}) copy-start(s32[2,16384]{1,0:T(2,128)} %param.11) | copy-start | bytes 393220
  12.1 14.5 %copy-start.2 = (bf16[16,32,128]{2,1,0:T(8,128)(2,1)S(1)}, bf16[16,32,128]{2,1,0:T(8,128)(2,1)}, u32[]{:S(2)}) copy-start(bf16[16,32,128]{2,1,0:T(8,128)(2,1)} %get-tuple-element.10) | copy-start | bytes 393220
  12.1 12.1 %collective-permute-start.5 = (bf16[16,32,128]{2,1,0:T(8,128)(2,1)}, bf16[16,32,128]{2,1,0:T(8,128)(2,1)S(1)}, u32[]{:S(2)}, u32[]{:S(2)}) collective-permute-start(bf16[16,32,128]{2,1,0:T(8,128)(2,1)} %get-tuple-element.10), channel_id=1, source_target_pairs={{0,1},{1,2},{2,3},{3,0},{4,5},{5,6},{6,7},{7,4},{8,9},{9,10},{10,1... | collective-permute-start | bytes 393224 | tf_op jit(solution)/shard_map/ppermute | solution.py:397
  15.2 11.5 %collective-permute-start.6 = (bf16[16,32,128]{2,1,0:T(8,128)(2,1)}, bf16[16,32,128]{2,1,0:T(8,128)(2,1)S(1)}, u32[]{:S(2)}, u32[]{:S(2)}) collective-permute-start(bf16[16,32,128]{2,1,0:T(8,128)(2,1)} %get-tuple-element.10), channel_id=1, source_target_pairs={{0,2},{1,3},{2,0},{3,1},{4,6},{5,7},{6,4},{7,5},{8,10},{9,11},{10,... | collective-permute-start | bytes 393224 | tf_op jit(solution)/shard_map/ppermute | solution.py:397
  17.8 8.9 %collective-permute-start.7 = (bf16[16,32,128]{2,1,0:T(8,128)(2,1)}, bf16[16,32,128]{2,1,0:T(8,128)(2,1)S(1)}, u32[]{:S(2)}, u32[]{:S(2)}) collective-permute-start(bf16[16,32,128]{2,1,0:T(8,128)(2,1)} %get-tuple-element.10), channel_id=1, source_target_pairs={{0,3},{1,0},{2,1},{3,2},{4,7},{5,4},{6,5},{7,6},{8,11},{9,8},{10,9... | collective-permute-start | bytes 393224 | tf_op jit(solution)/shard_map/ppermute | solution.py:397
  19.2 9.1 %copy-start.4 = (s32[128,9]{0,1:T(8,128)S(1)}, s32[128,9]{0,1:T(8,128)}, u32[]{:S(2)}) copy-start(s32[128,9]{0,1:T(8,128)} %param.12) | copy-start | bytes 13828
  19.3 10.7 %copy-start.3 = (s32[32,27]{1,0:T(8,128)S(1)}, s32[32,27]{1,0:T(8,128)}, u32[]{:S(2)}) copy-start(s32[32,27]{1,0:T(8,128)} %param.14) | copy-start | bytes 10372
  19.4 11.5 %copy-start.5 = (s32[128,8]{0,1:T(8,128)S(1)}, s32[128,8]{0,1:T(8,128)}, u32[]{:S(2)}) copy-start(s32[128,8]{0,1:T(8,128)} %param.13) | copy-start | bytes 12292
  19.4 29.3 %collective-permute-start = (bf16[32,17408]{1,0:T(8,128)(2,1)S(1)}, bf16[32,17408]{1,0:T(8,128)(2,1)}, u32[]{:S(2)}, u32[]{:S(2)}) collective-permute-start(bf16[32,17408]{1,0:T(8,128)(2,1)S(1)} %constant_dynamic-update-slice_fusion), channel_id=1, source_target_pairs={{0,1},{1,2},{2,3},{3,4},{4,5},{5,6},{6,7},{7,8},{8,9},{9,10},{10,1... | collective-permute-start | bytes 3342344 | tf_op jit(solution)/shard_map/ppermute | solution.py:435
  23.0 51.4 %collective-permute-start.1 = (bf16[32,17408]{1,0:T(8,128)(2,1)S(1)}, bf16[32,17408]{1,0:T(8,128)(2,1)}, u32[]{:S(2)}, u32[]{:S(2)}) collective-permute-start(bf16[32,17408]{1,0:T(8,128)(2,1)S(1)} %constant_dynamic-update-slice_fusion), channel_id=1, source_target_pairs={{1,0},{2,1},{3,2},{4,3},{5,4},{6,5},{7,6},{8,7},{9,8},{10,9},{11,1... | collective-permute-start | bytes 3342344 | tf_op jit(solution)/shard_map/ppermute | solution.py:436
  31.6 42.8 %copy-start.6 = (bf16[32,32,256]{2,1,0:T(8,128)(2,1)S(1)}, bf16[32,32,256]{2,1,0:T(8,128)(2,1)}, u32[]{:S(2)}) copy-start(bf16[32,32,256]{2,1,0:T(8,128)(2,1)} %get-tuple-element.9.rest_0_) | copy-start | bytes 1572868
  74.4 46.6 %collective-permute-start.2 = (bf16[32,32,256]{2,1,0:T(8,128)(2,1)S(1)}, bf16[32,32,256]{2,1,0:T(8,128)(2,1)S(1)}, u32[]{:S(2)}, u32[]{:S(2)}) collective-permute-start(bf16[32,32,256]{2,1,0:T(8,128)(2,1)S(1)} %copy-done.6), channel_id=1, source_target_pairs={{0,1},{1,2},{2,3},{3,0},{4,5},{5,6},{6,7},{7,4},{8,9},{9,10},{10,1... | collective-permute-start | bytes 1572872 | tf_op jit(solution)/shard_map/ppermute | solution.py:406
  77.8 43.3 %collective-permute-start.3 = (bf16[32,32,256]{2,1,0:T(8,128)(2,1)S(1)}, bf16[32,32,256]{2,1,0:T(8,128)(2,1)S(1)}, u32[]{:S(2)}, u32[]{:S(2)}) collective-permute-start(bf16[32,32,256]{2,1,0:T(8,128)(2,1)S(1)} %copy-done.6), channel_id=1, source_target_pairs={{0,2},{1,3},{2,0},{3,1},{4,6},{5,7},{6,4},{7,5},{8,10},{9,11},{10,... | collective-permute-start | bytes 1572872 | tf_op jit(solution)/shard_map/ppermute | solution.py:406
  77.8 43.3 %collective-permute-start.4 = (bf16[32,32,256]{2,1,0:T(8,128)(2,1)S(1)}, bf16[32,32,256]{2,1,0:T(8,128)(2,1)S(1)}, u32[]{:S(2)}, u32[]{:S(2)}) collective-permute-start(bf16[32,32,256]{2,1,0:T(8,128)(2,1)S(1)} %copy-done.6), channel_id=1, source_target_pairs={{0,3},{1,0},{2,1},{3,2},{4,7},{5,4},{6,5},{7,6},{8,11},{9,8},{10,9... | collective-permute-start | bytes 1572872 | tf_op jit(solution)/shard_map/ppermute | solution.py:406
  121.1 0.8 copy-start.7
  121.1 1.0 copy-start.8
  122.0 0.8 copy-start.9
Sparse Core Ops, SparseCore 0:
  27.7 66.9 all-gather.1

commit v4 on v3

--- a/solution.py
+++ b/solution.py
@@ -103,31 +103,26 @@
 
 
 def scatter_row(charge_ref, base, x_ref, cells_ref):
-    sides = x_ref.shape[0]
-
     def group(first, carry):
         for extra in range(8):
             t = first * 8 + extra
             hot = one_hot(cells_ref[pl.ds(t, 1), :])
             y = dot(x_ref[:, pl.ds(pl.multiple_of(t * 128, 128), 128)], hot, NT)
-            high, low = split(y)
-            charge_ref[base + t, :sides] = high
-            charge_ref[base + t, sides:] = low
+            charge_ref[base + t] = y.astype(jnp.bfloat16)
         return carry
 
     lax.fori_loop(0, cells_ref.shape[0] // 8, group, 0)
 
 
 def grid_field(index_ref, charge_ref, lhs_ref, table_ref, first, step):
-    sides = charge_ref.shape[1] // 2
+    sides = charge_ref.shape[1]
     slots = table_ref.shape[0] // CELLS
     for t in range(step):
         for k in range(slots):
-            lhs_ref[t * 2 * sides : (t + 1) * 2 * sides, k * CELLS : (k + 1) * CELLS] = charge_ref[
+            lhs_ref[t * sides : (t + 1) * sides, k * CELLS : (k + 1) * CELLS] = charge_ref[
                 index_ref[(first + t) * slots + k]
             ]
-    u = dot(lhs_ref[...], table_ref[...], NN).reshape(step, 2 * sides, CELLS)
-    return u[:, :sides] + u[:, sides:]
+    return dot(lhs_ref[...], table_ref[...], NN).reshape(step, sides, CELLS)
 
 
 def near_own_kernel(index_ref, x_ref, cells_ref, table_ref, u_ref, charge_ref, lhs_ref):
@@ -157,8 +152,8 @@
         out_specs=pl.BlockSpec((step, sides, CELLS), lambda g: (g, 0, 0)),
         out_shape=jax.ShapeDtypeStruct((leaves, sides, CELLS), jnp.float32),
         scratch_shapes=[
-            pltpu.VMEM((leaves + 1, 2 * sides, CELLS), jnp.bfloat16),
-            pltpu.VMEM((step * 2 * sides, table.shape[0]), jnp.bfloat16),
+            pltpu.VMEM((leaves + 1, sides, CELLS), jnp.bfloat16),
+            pltpu.VMEM((step * sides, table.shape[0]), jnp.bfloat16),
         ],
         compiler_params=pltpu.CompilerParams(vmem_limit_bytes=VMEM_LIMIT),
         cost_estimate=pl.CostEstimate(
@@ -209,8 +204,8 @@
         out_specs=pl.BlockSpec((sides, step * 128), lambda g: (0, g)),
         out_shape=jax.ShapeDtypeStruct((sides, leaves * 128), jnp.float32),
         scratch_shapes=[
-            pltpu.VMEM((2 * leaves + 1, 2 * sides, CELLS), jnp.bfloat16),
-            pltpu.VMEM((step * 2 * sides, table.shape[0]), jnp.bfloat16),
+            pltpu.VMEM((2 * leaves + 1, sides, CELLS), jnp.bfloat16),
+            pltpu.VMEM((step * sides, table.shape[0]), jnp.bfloat16),
         ],
         compiler_params=pltpu.CompilerParams(vmem_limit_bytes=VMEM_LIMIT),
         cost_estimate=pl.CostEstimate(

time: 145 us -> 145 us (level); the launches traced: 145 us -> 142 us
  Pallas kernels: 70.2 us -> 65.8 us
  waiting for transfers between devices: 33.7 us -> 35.4 us
    pallas_call x1, Pallas kernels: 21.8 us -> 19 us  [near_rest(): pl.pallas_call(near_rest_kernel, grid=(leaves // step,), in_specs=[pl.Blo...]
    pallas_call x1, Pallas kernels: 11.5 us -> 9.83 us  [near_own(): pl.pallas_call(near_own_kernel, grid=(leaves // step,), in_specs=[pl.Bloc...]
    ppermute x1, waiting for transfers between devices: 5.56 us -> 7.22 us  [body(): before = lax.ppermute(packed, everyone, upward)]
  transfers between devices with their start and end apart: 9 -> 9, of which waited for: 3 -> 3; matrix products, arithmetic and copies ran while one was open for 6% -> 6% of each run, Pallas kernels for 34% -> 32%
where the time goes in v4:
time: 145 us; the launch traced here: 142 us
  Pallas kernels  65.8 us (45%)
  waiting for transfers between devices  35.4 us (24%)
  starting transfers between devices  17.6 us (12%)
  between operations  13.5 us (9%)
  local copies, waits for them, and re-layouts  6.35 us (4%)
  other arithmetic  3.51 us (2%)
    ppermute x1, waiting for transfers between devices, body(): after = lax.ppermute(packed, everyone, downward)  25.7 us
    pallas_call x1, Pallas kernels, near_rest(): pl.pallas_call(near_rest_kernel, grid=(leaves // step,), in_specs=[pl.Blo...  19 us
    pallas_call x1, Pallas kernels, parents_down(): pl.pallas_call(functools.partial(parent_kernel, len(pieces)), grid=(paren...  16 us
    pallas_call x1, Pallas kernels, finish(): pl.pallas_call(functools.partial(final_kernel, len(pieces)), grid=(leaves...  15.3 us
    pallas_call x1, Pallas kernels, near_own(): pl.pallas_call(near_own_kernel, grid=(leaves // step,), in_specs=[pl.Bloc...  9.83 us
    ppermute x1, waiting for transfers between devices, body(): before = lax.ppermute(packed, everyone, upward)  7.22 us
    ppermute x3, starting transfers between devices, gather_parents(): line.append(lax.ppermute(pairs, 'sib', turn))  7 us
    ppermute x3, starting transfers between devices, gather_leaves(): lax.ppermute(block, 'sib', [(i, (i + shift) % sibs) for i in range(sibs)])  5.74 us
  transfers between devices with their start and end apart: 9, of which 3 were waited for; matrix products, arithmetic and copies ran while one was open for 6% of the time, Pallas kernels for 32%

profile of v4, /device:TPU:0, one launch (start us, length us, event | category | flops | bytes accessed | tf_op | source)
XLA Modules:
  0.0 142.1 jit_solution(8783026952714325452)
XLA Ops:
  6.5 0.0 copy-start
  6.5 0.0 all-gather.2.cloned.1.call-start
  6.5 5.6 %coefficients.1 = (bf16[32,32,256]{2,1,0:T(8,128)(2,1)}, bf16[16,32,128]{2,1,0:T(8,128)(2,1)}) custom-call(bf16[32,16384]{1,0:T(8,128)(2,1)} %x_ref.3, bf16[128,64,128]{2,1,0:T(8,128)(2,1)} %rest_6_.1, bf16[32,64,256]{2,1,0:T(8,128)(2,1)} %rest_2_.1), custom_call_target="tpu_custom_call" | custom-call | flops 1000000 | bytes 1000 | tf_op jit(solution)/shard_map/coefficients/pallas_call | solution.py:81
  12.1 0.0 copy-start.1
  12.1 0.0 copy-start.2
  12.1 3.1 %collective-permute-start.5 = (bf16[16,32,128]{2,1,0:T(8,128)(2,1)}, bf16[16,32,128]{2,1,0:T(8,128)(2,1)S(1)}, u32[]{:S(2)}, u32[]{:S(2)}) collective-permute-start(bf16[16,32,128]{2,1,0:T(8,128)(2,1)} %get-tuple-element.10), channel_id=1, source_target_pairs={{0,1},{1,2},{2,3},{3,0},{4,5},{5,6},{6,7},{7,4},{8,9},{9,10},{10,1... | collective-permute-start | bytes 393224 | tf_op jit(solution)/shard_map/ppermute | solution.py:392
  15.2 2.6 %collective-permute-start.6 = (bf16[16,32,128]{2,1,0:T(8,128)(2,1)}, bf16[16,32,128]{2,1,0:T(8,128)(2,1)S(1)}, u32[]{:S(2)}, u32[]{:S(2)}) collective-permute-start(bf16[16,32,128]{2,1,0:T(8,128)(2,1)} %get-tuple-element.10), channel_id=1, source_target_pairs={{0,2},{1,3},{2,0},{3,1},{4,6},{5,7},{6,4},{7,5},{8,10},{9,11},{10,... | collective-permute-start | bytes 393224 | tf_op jit(solution)/shard_map/ppermute | solution.py:392
  17.8 1.3 collective-permute-start.7
  19.1 0.0 copy-done
  19.1 0.1 constant_dynamic-update-slice_fusion.1
  19.2 0.0 copy-done.1
  19.2 0.0 copy-start.4
  19.3 0.0 copy-start.3
  19.4 0.0 copy-start.5
  19.4 3.6 %collective-permute-start = (bf16[32,17408]{1,0:T(8,128)(2,1)S(1)}, bf16[32,17408]{1,0:T(8,128)(2,1)}, u32[]{:S(2)}, u32[]{:S(2)}) collective-permute-start(bf16[32,17408]{1,0:T(8,128)(2,1)S(1)} %constant_dynamic-update-slice_fusion), channel_id=1, source_target_pairs={{0,1},{1,2},{2,3},{3,4},{4,5},{5,6},{6,7},{7,8},{8,9},{9,10},{10,1... | collective-permute-start | bytes 3342344 | tf_op jit(solution)/shard_map/ppermute | solution.py:430
  23.0 1.3 collective-permute-start.1
  24.3 0.0 collective-permute-done.5
  24.3 2.4 %collective-permute-done.6 = bf16[16,32,128]{2,1,0:T(8,128)(2,1)S(1)} collective-permute-done((bf16[16,32,128]{2,1,0:T(8,128)(2,1)}, bf16[16,32,128]{2,1,0:T(8,128)(2,1)S(1)}, u32[]{:S(2)}, u32[]{:S(2)}) %collective-permute-start.6) | collective-permute-done | bytes 131104 | tf_op jit(solution)/shard_map/ppermute | solution.py:392
  26.7 0.0 collective-permute-done.7
  26.7 0.0 copy-done.2
  26.7 0.9 pad_maximum_fusion
  27.5 0.0 all-gather.2.cloned.1.call-update
  27.6 0.7 slice_add_fusion.2
  28.3 0.0 copy-done.4
  28.3 0.1 fusion.16
  28.4 0.1 copy.15
  28.5 0.7 select_n.69.index_ref
  29.2 0.1 copy.16
  29.3 0.7 reshape.54.index_ref
  30.1 0.0 copy-done.3
  30.1 0.7 reshape.53.index_ref
  30.8 0.0 copy-done.5
  30.9 0.1 copy.14
  31.0 0.7 reshape.51.index_ref
  31.6 0.0 copy-start.6
  31.6 9.8 %near_own.1.u_ref = f32[128,32,256]{2,1,0:T(8,128)} custom-call(s32[384]{0:T(512)} %reshape.54.index_ref, bf16[32,16384]{1,0:T(8,128)(2,1)} %x_ref.3, s32[128,128]{1,0:T(8,128)} %bitcast.1, bf16[768,256]{1,0:T(8,128)(2,1)} %constant.120.table_ref), custom_call_target="tpu_custom_call" | custom-call | flops 1000000 | bytes 1000 | tf_op jit(solution)/shard_map/near_own/pallas_call | solution.py:143
  41.5 7.2 %collective-permute-done.above_ref = bf16[32,17408]{1,0:T(8,128)(2,1)} collective-permute-done((bf16[32,17408]{1,0:T(8,128)(2,1)S(1)}, bf16[32,17408]{1,0:T(8,128)(2,1)}, u32[]{:S(2)}, u32[]{:S(2)}) %collective-permute-start) | collective-permute-done | bytes 1114144 | tf_op jit(solution)/shard_map/ppermute | solution.py:430
  48.7 25.7 %collective-permute-done.1.below_ref = bf16[32,17408]{1,0:T(8,128)(2,1)} collective-permute-done((bf16[32,17408]{1,0:T(8,128)(2,1)S(1)}, bf16[32,17408]{1,0:T(8,128)(2,1)}, u32[]{:S(2)}, u32[]{:S(2)}) %collective-permute-start.1) | collective-permute-done | bytes 1114144 | tf_op jit(solution)/shard_map/ppermute | solution.py:431
  74.4 0.0 copy-done.6
  74.4 3.4 %collective-permute-start.2 = (bf16[32,32,256]{2,1,0:T(8,128)(2,1)S(1)}, bf16[32,32,256]{2,1,0:T(8,128)(2,1)S(1)}, u32[]{:S(2)}, u32[]{:S(2)}) collective-permute-start(bf16[32,32,256]{2,1,0:T(8,128)(2,1)S(1)} %copy-done.6), channel_id=1, source_target_pairs={{0,1},{1,2},{2,3},{3,0},{4,5},{5,6},{6,7},{7,4},{8,9},{9,10},{10,1... | collective-permute-start | bytes 1572872 | tf_op jit(solution)/shard_map/ppermute | solution.py:401
  77.8 0.0 collective-permute-start.3
  77.8 2.4 %collective-permute-start.4 = (bf16[32,32,256]{2,1,0:T(8,128)(2,1)S(1)}, bf16[32,32,256]{2,1,0:T(8,128)(2,1)S(1)}, u32[]{:S(2)}, u32[]{:S(2)}) collective-permute-start(bf16[32,32,256]{2,1,0:T(8,128)(2,1)S(1)} %copy-done.6), channel_id=1, source_target_pairs={{0,3},{1,0},{2,1},{3,2},{4,7},{5,4},{6,5},{7,6},{8,11},{9,8},{10,9... | collective-permute-start | bytes 1572872 | tf_op jit(solution)/shard_map/ppermute | solution.py:401
  80.2 0.9 slice_convert_fusion.1
  81.0 0.6 add.125.cells_above_ref
  81.7 0.9 slice_convert_fusion
  82.5 0.6 add.127.cells_below_ref
  83.2 19.0 %near_rest.1.rest_7_ = f32[32,16384]{1,0:T(8,128)} custom-call(s32[768]{0:T(1024)} %select_n.69.index_ref, bf16[32,17408]{1,0:T(8,128)(2,1)} %collective-permute-done.above_ref, bf16[32,17408]{1,0:T(8,128)(2,1)} %collective-permute-done.1.below_ref, s32[128,128]{1,0:T(8,128)} %add.125.cells_above_ref, s32[128,128]{1,0:T(8,128)} %add.127.cells_below_ref, ...), custom_call_target="tpu_custom_call" | custom-call | flops 24999999488 | bytes 1000 | tf_op jit(solution)/shard_map/near_rest/pallas_call | solution.py:191
  102.2 0.0 all-gather.2.cloned.1.call-done.rest_0_
  102.2 16.0 %parents_down.1.rest_5_ = f32[32,32,256]{2,1,0:T(8,128)} custom-call(s32[864]{0:T(1024)} %reshape.53.index_ref, bf16[512,32,128]{2,1,0:T(8,128)(2,1)} %all-gather.2.cloned.1.call-done.rest_0_, bf16[32,64,1728]{2,1,0:T(8,128)(2,1)} %rest_1_.1, bf16[32,64,256]{2,1,0:T(8,128)(2,1)} %rest_2_.1), custom_call_target="tpu_custom_call" | custom-call | flops 16999999488 | bytes 1000 | tf_op jit(solution)/shard_map/parents_down/pallas_call | solution.py:281
  118.2 0.0 collective-permute-done.2.rest_1_
  118.2 0.0 copy-start.7
  118.2 0.0 collective-permute-done.3.rest_2_
  118.3 0.0 copy-start.8
  118.3 0.0 collective-permute-done.4.rest_3_
  118.3 0.8 copy-done.7
  119.0 0.2 copy-done.8
  119.2 0.0 copy-start.9
  119.2 0.8 copy-done.9
  120.0 15.3 %finish.1 = f32[32,16384]{1,0:T(8,128)} custom-call(s32[1024]{0:T(1024)} %reshape.51.index_ref, bf16[32,32,256]{2,1,0:T(8,128)(2,1)} %get-tuple-element.9.rest_0_, bf16[32,32,256]{2,1,0:T(8,128)(2,1)} %copy-done.7, bf16[32,32,256]{2,1,0:T(8,128)(2,1)} %copy-done.8, bf16[32,32,256]{2,1,0:T(8,128)(2,1)} %copy-done.9, bf16[128,64,512]{2,1,0:T(8,128)(2,1)} %rest_4_.1, ...), custom_call_target="tpu_custom_call" | custom-call | flops 17999998976 | bytes 1000 | tf_op jit(solution)/shard_map/finish/pallas_call | solution.py:362
  (10 shorter events, 0.2 us)
Async XLA Ops:
  6.5 12.6 %copy-start = (bf16[32,16384]{1,0:T(8,128)(2,1)S(1)}, bf16[32,16384]{1,0:T(8,128)(2,1)}, u32[]{:S(2)}) copy-start(bf16[32,16384]{1,0:T(8,128)(2,1)} %x_ref.3) | copy-start | bytes 3145732
  6.5 95.7 %all-gather.2.cloned.1.call-start = ((), (), s32[]{:S(2)}) async-start(), calls=%async_computation | async-start | bytes 4718592 | tf_op jit(solution)/shard_map/all_gather | solution.py:394
  12.1 7.1 %copy-start.1 = (s32[2,16384]{1,0:T(2,128)S(1)}, s32[2,16384]{1,0:T(2,128)}, u32[]{:S(2)}) copy-start(s32[2,16384]{1,0:T(2,128)} %param.11) | copy-start | bytes 393220
  12.1 14.5 %copy-start.2 = (bf16[16,32,128]{2,1,0:T(8,128)(2,1)S(1)}, bf16[16,32,128]{2,1,0:T(8,128)(2,1)}, u32[]{:S(2)}) copy-start(bf16[16,32,128]{2,1,0:T(8,128)(2,1)} %get-tuple-element.10) | copy-start | bytes 393220
  12.1 12.1 %collective-permute-start.5 = (bf16[16,32,128]{2,1,0:T(8,128)(2,1)}, bf16[16,32,128]{2,1,0:T(8,128)(2,1)S(1)}, u32[]{:S(2)}, u32[]{:S(2)}) collective-permute-start(bf16[16,32,128]{2,1,0:T(8,128)(2,1)} %get-tuple-element.10), channel_id=1, source_target_pairs={{0,1},{1,2},{2,3},{3,0},{4,5},{5,6},{6,7},{7,4},{8,9},{9,10},{10,1... | collective-permute-start | bytes 393224 | tf_op jit(solution)/shard_map/ppermute | solution.py:392
  15.2 11.5 %collective-permute-start.6 = (bf16[16,32,128]{2,1,0:T(8,128)(2,1)}, bf16[16,32,128]{2,1,0:T(8,128)(2,1)S(1)}, u32[]{:S(2)}, u32[]{:S(2)}) collective-permute-start(bf16[16,32,128]{2,1,0:T(8,128)(2,1)} %get-tuple-element.10), channel_id=1, source_target_pairs={{0,2},{1,3},{2,0},{3,1},{4,6},{5,7},{6,4},{7,5},{8,10},{9,11},{10,... | collective-permute-start | bytes 393224 | tf_op jit(solution)/shard_map/ppermute | solution.py:392
  17.8 8.9 %collective-permute-start.7 = (bf16[16,32,128]{2,1,0:T(8,128)(2,1)}, bf16[16,32,128]{2,1,0:T(8,128)(2,1)S(1)}, u32[]{:S(2)}, u32[]{:S(2)}) collective-permute-start(bf16[16,32,128]{2,1,0:T(8,128)(2,1)} %get-tuple-element.10), channel_id=1, source_target_pairs={{0,3},{1,0},{2,1},{3,2},{4,7},{5,4},{6,5},{7,6},{8,11},{9,8},{10,9... | collective-permute-start | bytes 393224 | tf_op jit(solution)/shard_map/ppermute | solution.py:392
  19.2 9.1 %copy-start.4 = (s32[128,9]{0,1:T(8,128)S(1)}, s32[128,9]{0,1:T(8,128)}, u32[]{:S(2)}) copy-start(s32[128,9]{0,1:T(8,128)} %param.12) | copy-start | bytes 13828
  19.3 10.7 %copy-start.3 = (s32[32,27]{1,0:T(8,128)S(1)}, s32[32,27]{1,0:T(8,128)}, u32[]{:S(2)}) copy-start(s32[32,27]{1,0:T(8,128)} %param.14) | copy-start | bytes 10372
  19.4 11.5 %copy-start.5 = (s32[128,8]{0,1:T(8,128)S(1)}, s32[128,8]{0,1:T(8,128)}, u32[]{:S(2)}) copy-start(s32[128,8]{0,1:T(8,128)} %param.13) | copy-start | bytes 12292
  19.4 29.3 %collective-permute-start = (bf16[32,17408]{1,0:T(8,128)(2,1)S(1)}, bf16[32,17408]{1,0:T(8,128)(2,1)}, u32[]{:S(2)}, u32[]{:S(2)}) collective-permute-start(bf16[32,17408]{1,0:T(8,128)(2,1)S(1)} %constant_dynamic-update-slice_fusion), channel_id=1, source_target_pairs={{0,1},{1,2},{2,3},{3,4},{4,5},{5,6},{6,7},{7,8},{8,9},{9,10},{10,1... | collective-permute-start | bytes 3342344 | tf_op jit(solution)/shard_map/ppermute | solution.py:430
  23.0 51.4 %collective-permute-start.1 = (bf16[32,17408]{1,0:T(8,128)(2,1)S(1)}, bf16[32,17408]{1,0:T(8,128)(2,1)}, u32[]{:S(2)}, u32[]{:S(2)}) collective-permute-start(bf16[32,17408]{1,0:T(8,128)(2,1)S(1)} %constant_dynamic-update-slice_fusion), channel_id=1, source_target_pairs={{1,0},{2,1},{3,2},{4,3},{5,4},{6,5},{7,6},{8,7},{9,8},{10,9},{11,1... | collective-permute-start | bytes 3342344 | tf_op jit(solution)/shard_map/ppermute | solution.py:431
  31.6 42.8 %copy-start.6 = (bf16[32,32,256]{2,1,0:T(8,128)(2,1)S(1)}, bf16[32,32,256]{2,1,0:T(8,128)(2,1)}, u32[]{:S(2)}) copy-start(bf16[32,32,256]{2,1,0:T(8,128)(2,1)} %get-tuple-element.9.rest_0_) | copy-start | bytes 1572868
  74.4 43.8 %collective-permute-start.2 = (bf16[32,32,256]{2,1,0:T(8,128)(2,1)S(1)}, bf16[32,32,256]{2,1,0:T(8,128)(2,1)S(1)}, u32[]{:S(2)}, u32[]{:S(2)}) collective-permute-start(bf16[32,32,256]{2,1,0:T(8,128)(2,1)S(1)} %copy-done.6), channel_id=1, source_target_pairs={{0,1},{1,2},{2,3},{3,0},{4,5},{5,6},{6,7},{7,4},{8,9},{9,10},{10,1... | collective-permute-start | bytes 1572872 | tf_op jit(solution)/shard_map/ppermute | solution.py:401
  77.8 40.5 %collective-permute-start.3 = (bf16[32,32,256]{2,1,0:T(8,128)(2,1)S(1)}, bf16[32,32,256]{2,1,0:T(8,128)(2,1)S(1)}, u32[]{:S(2)}, u32[]{:S(2)}) collective-permute-start(bf16[32,32,256]{2,1,0:T(8,128)(2,1)S(1)} %copy-done.6), channel_id=1, source_target_pairs={{0,2},{1,3},{2,0},{3,1},{4,6},{5,7},{6,4},{7,5},{8,10},{9,11},{10,... | collective-permute-start | bytes 1572872 | tf_op jit(solution)/shard_map/ppermute | solution.py:401
  77.8 40.5 %collective-permute-start.4 = (bf16[32,32,256]{2,1,0:T(8,128)(2,1)S(1)}, bf16[32,32,256]{2,1,0:T(8,128)(2,1)S(1)}, u32[]{:S(2)}, u32[]{:S(2)}) collective-permute-start(bf16[32,32,256]{2,1,0:T(8,128)(2,1)S(1)} %copy-done.6), channel_id=1, source_target_pairs={{0,3},{1,0},{2,1},{3,2},{4,7},{5,4},{6,5},{7,6},{8,11},{9,8},{10,9... | collective-permute-start | bytes 1572872 | tf_op jit(solution)/shard_map/ppermute | solution.py:401
  118.2 0.8 copy-start.7
  118.3 1.0 copy-start.8
  119.2 0.8 copy-start.9
Sparse Core Ops, SparseCore 0:
  27.7 66.8 all-gather.1

commit v5 on v3

--- a/solution.py
+++ b/solution.py
@@ -77,7 +77,7 @@
 
 def coefficients(x, basis, transfer):
     sides, parents = x.shape[0], transfer.shape[0]
-    step = 8
+    step = 16
     return pl.pallas_call(
         coef_kernel,
         grid=(parents // step,),

time: 145 us -> 145 us (level)
  no operation moved by 1% of the time
where the time goes in v5:
time: 145 us; the launch traced here: 144 us
  Pallas kernels  69.7 us (48%)
  waiting for transfers between devices  33.7 us (23%)
  starting transfers between devices  17.6 us (12%)
  between operations  13.5 us (9%)
  local copies, waits for them, and re-layouts  6.35 us (4%)
  other arithmetic  3.51 us (2%)
    ppermute x1, waiting for transfers between devices, body(): after = lax.ppermute(packed, everyone, downward)  25.7 us
    pallas_call x1, Pallas kernels, near_rest(): pl.pallas_call(near_rest_kernel, grid=(leaves // step,), in_specs=[pl.Blo...  21.8 us
    pallas_call x1, Pallas kernels, parents_down(): pl.pallas_call(functools.partial(parent_kernel, len(pieces)), grid=(paren...  16 us
    pallas_call x1, Pallas kernels, finish(): pl.pallas_call(functools.partial(final_kernel, len(pieces)), grid=(leaves...  15.3 us
    pallas_call x1, Pallas kernels, near_own(): pl.pallas_call(near_own_kernel, grid=(leaves // step,), in_specs=[pl.Bloc...  11.5 us
    ppermute x3, starting transfers between devices, gather_parents(): line.append(lax.ppermute(pairs, 'sib', turn))  7 us
    ppermute x3, starting transfers between devices, gather_leaves(): lax.ppermute(block, 'sib', [(i, (i + shift) % sibs) for i in range(sibs)])  5.74 us
    ppermute x1, waiting for transfers between devices, body(): before = lax.ppermute(packed, everyone, upward)  5.56 us
  transfers between devices with their start and end apart: 9, of which 3 were waited for; matrix products, arithmetic and copies ran while one was open for 6% of the time, Pallas kernels for 34%

profile of v5, /device:TPU:0, one launch (start us, length us, event | category | flops | bytes accessed | tf_op | source)
XLA Modules:
  0.0 144.4 jit_solution(9420467742561496990)
XLA Ops:
  6.5 0.0 copy-start
  6.5 0.0 all-gather.2.cloned.1.call-start
  6.5 5.1 %coefficients.1 = (bf16[32,32,256]{2,1,0:T(8,128)(2,1)}, bf16[16,32,128]{2,1,0:T(8,128)(2,1)}) custom-call(bf16[32,16384]{1,0:T(8,128)(2,1)} %x_ref.3, bf16[128,64,128]{2,1,0:T(8,128)(2,1)} %rest_6_.1, bf16[32,64,256]{2,1,0:T(8,128)(2,1)} %rest_2_.1), custom_call_target="tpu_custom_call" | custom-call | flops 1000000 | bytes 1000 | tf_op jit(solution)/shard_map/coefficients/pallas_call | solution.py:81
  11.6 0.0 copy-start.1
  11.6 0.0 copy-start.2
  11.6 3.1 %collective-permute-start.5 = (bf16[16,32,128]{2,1,0:T(8,128)(2,1)}, bf16[16,32,128]{2,1,0:T(8,128)(2,1)S(1)}, u32[]{:S(2)}, u32[]{:S(2)}) collective-permute-start(bf16[16,32,128]{2,1,0:T(8,128)(2,1)} %get-tuple-element.10), channel_id=1, source_target_pairs={{0,1},{1,2},{2,3},{3,0},{4,5},{5,6},{6,7},{7,4},{8,9},{9,10},{10,1... | collective-permute-start | bytes 393224 | tf_op jit(solution)/shard_map/ppermute | solution.py:397
  14.7 2.6 %collective-permute-start.6 = (bf16[16,32,128]{2,1,0:T(8,128)(2,1)}, bf16[16,32,128]{2,1,0:T(8,128)(2,1)S(1)}, u32[]{:S(2)}, u32[]{:S(2)}) collective-permute-start(bf16[16,32,128]{2,1,0:T(8,128)(2,1)} %get-tuple-element.10), channel_id=1, source_target_pairs={{0,2},{1,3},{2,0},{3,1},{4,6},{5,7},{6,4},{7,5},{8,10},{9,11},{10,... | collective-permute-start | bytes 393224 | tf_op jit(solution)/shard_map/ppermute | solution.py:397
  17.3 1.3 collective-permute-start.7
  18.6 0.0 copy-done
  18.6 0.1 constant_dynamic-update-slice_fusion.1
  18.7 0.0 copy-done.1
  18.7 0.0 copy-start.4
  18.8 0.0 copy-start.3
  18.8 0.0 copy-start.5
  18.9 3.6 %collective-permute-start = (bf16[32,17408]{1,0:T(8,128)(2,1)S(1)}, bf16[32,17408]{1,0:T(8,128)(2,1)}, u32[]{:S(2)}, u32[]{:S(2)}) collective-permute-start(bf16[32,17408]{1,0:T(8,128)(2,1)S(1)} %constant_dynamic-update-slice_fusion), channel_id=1, source_target_pairs={{0,1},{1,2},{2,3},{3,4},{4,5},{5,6},{6,7},{7,8},{8,9},{9,10},{10,1... | collective-permute-start | bytes 3342344 | tf_op jit(solution)/shard_map/ppermute | solution.py:435
  22.5 1.3 collective-permute-start.1
  23.7 0.0 collective-permute-done.5
  23.7 2.4 %collective-permute-done.6 = bf16[16,32,128]{2,1,0:T(8,128)(2,1)S(1)} collective-permute-done((bf16[16,32,128]{2,1,0:T(8,128)(2,1)}, bf16[16,32,128]{2,1,0:T(8,128)(2,1)S(1)}, u32[]{:S(2)}, u32[]{:S(2)}) %collective-permute-start.6) | collective-permute-done | bytes 131104 | tf_op jit(solution)/shard_map/ppermute | solution.py:397
  26.2 0.0 collective-permute-done.7
  26.2 0.0 copy-done.2
  26.2 0.9 pad_maximum_fusion
  27.0 0.0 all-gather.2.cloned.1.call-update
  27.1 0.7 slice_add_fusion.2
  27.8 0.0 copy-done.4
  27.8 0.1 fusion.16
  27.9 0.1 copy.15
  28.0 0.7 select_n.69.index_ref
  28.7 0.1 copy.16
  28.8 0.7 reshape.54.index_ref
  29.6 0.0 copy-done.3
  29.6 0.7 reshape.53.index_ref
  30.3 0.0 copy-done.5
  30.3 0.1 copy.14
  30.4 0.7 reshape.51.index_ref
  31.1 0.0 copy-start.6
  31.1 11.5 %near_own.1.u_ref = f32[128,32,256]{2,1,0:T(8,128)} custom-call(s32[384]{0:T(512)} %reshape.54.index_ref, bf16[32,16384]{1,0:T(8,128)(2,1)} %x_ref.3, s32[128,128]{1,0:T(8,128)} %bitcast.1, bf16[768,256]{1,0:T(8,128)(2,1)} %constant.120.table_ref), custom_call_target="tpu_custom_call" | custom-call | flops 1000000 | bytes 1000 | tf_op jit(solution)/shard_map/near_own/pallas_call | solution.py:148
  42.6 5.6 %collective-permute-done.above_ref = bf16[32,17408]{1,0:T(8,128)(2,1)} collective-permute-done((bf16[32,17408]{1,0:T(8,128)(2,1)S(1)}, bf16[32,17408]{1,0:T(8,128)(2,1)}, u32[]{:S(2)}, u32[]{:S(2)}) %collective-permute-start) | collective-permute-done | bytes 1114144 | tf_op jit(solution)/shard_map/ppermute | solution.py:435
  48.2 25.7 %collective-permute-done.1.below_ref = bf16[32,17408]{1,0:T(8,128)(2,1)} collective-permute-done((bf16[32,17408]{1,0:T(8,128)(2,1)S(1)}, bf16[32,17408]{1,0:T(8,128)(2,1)}, u32[]{:S(2)}, u32[]{:S(2)}) %collective-permute-start.1) | collective-permute-done | bytes 1114144 | tf_op jit(solution)/shard_map/ppermute | solution.py:436
  73.9 0.0 copy-done.6
  73.9 3.4 %collective-permute-start.2 = (bf16[32,32,256]{2,1,0:T(8,128)(2,1)S(1)}, bf16[32,32,256]{2,1,0:T(8,128)(2,1)S(1)}, u32[]{:S(2)}, u32[]{:S(2)}) collective-permute-start(bf16[32,32,256]{2,1,0:T(8,128)(2,1)S(1)} %copy-done.6), channel_id=1, source_target_pairs={{0,1},{1,2},{2,3},{3,0},{4,5},{5,6},{6,7},{7,4},{8,9},{9,10},{10,1... | collective-permute-start | bytes 1572872 | tf_op jit(solution)/shard_map/ppermute | solution.py:406
  77.3 0.0 collective-permute-start.3
  77.3 2.4 %collective-permute-start.4 = (bf16[32,32,256]{2,1,0:T(8,128)(2,1)S(1)}, bf16[32,32,256]{2,1,0:T(8,128)(2,1)S(1)}, u32[]{:S(2)}, u32[]{:S(2)}) collective-permute-start(bf16[32,32,256]{2,1,0:T(8,128)(2,1)S(1)} %copy-done.6), channel_id=1, source_target_pairs={{0,3},{1,0},{2,1},{3,2},{4,7},{5,4},{6,5},{7,6},{8,11},{9,8},{10,9... | collective-permute-start | bytes 1572872 | tf_op jit(solution)/shard_map/ppermute | solution.py:406
  79.6 0.9 slice_convert_fusion.1
  80.5 0.6 add.125.cells_above_ref
  81.1 0.9 slice_convert_fusion
  82.0 0.6 add.127.cells_below_ref
  82.7 21.8 %near_rest.1.rest_7_ = f32[32,16384]{1,0:T(8,128)} custom-call(s32[768]{0:T(1024)} %select_n.69.index_ref, bf16[32,17408]{1,0:T(8,128)(2,1)} %collective-permute-done.above_ref, bf16[32,17408]{1,0:T(8,128)(2,1)} %collective-permute-done.1.below_ref, s32[128,128]{1,0:T(8,128)} %add.125.cells_above_ref, s32[128,128]{1,0:T(8,128)} %add.127.cells_below_ref, ...), custom_call_target="tpu_custom_call" | custom-call | flops 24999999488 | bytes 1000 | tf_op jit(solution)/shard_map/near_rest/pallas_call | solution.py:196
  104.5 0.0 all-gather.2.cloned.1.call-done.rest_0_
  104.5 16.0 %parents_down.1.rest_5_ = f32[32,32,256]{2,1,0:T(8,128)} custom-call(s32[864]{0:T(1024)} %reshape.53.index_ref, bf16[512,32,128]{2,1,0:T(8,128)(2,1)} %all-gather.2.cloned.1.call-done.rest_0_, bf16[32,64,1728]{2,1,0:T(8,128)(2,1)} %rest_1_.1, bf16[32,64,256]{2,1,0:T(8,128)(2,1)} %rest_2_.1), custom_call_target="tpu_custom_call" | custom-call | flops 16999999488 | bytes 1000 | tf_op jit(solution)/shard_map/parents_down/pallas_call | solution.py:286
  120.5 0.0 collective-permute-done.2.rest_1_
  120.5 0.0 copy-start.7
  120.5 0.0 collective-permute-done.3.rest_2_
  120.6 0.0 copy-start.8
  120.6 0.0 collective-permute-done.4.rest_3_
  120.6 0.8 copy-done.7
  121.3 0.2 copy-done.8
  121.5 0.0 copy-start.9
  121.5 0.8 copy-done.9
  122.3 15.3 %finish.1 = f32[32,16384]{1,0:T(8,128)} custom-call(s32[1024]{0:T(1024)} %reshape.51.index_ref, bf16[32,32,256]{2,1,0:T(8,128)(2,1)} %get-tuple-element.9.rest_0_, bf16[32,32,256]{2,1,0:T(8,128)(2,1)} %copy-done.7, bf16[32,32,256]{2,1,0:T(8,128)(2,1)} %copy-done.8, bf16[32,32,256]{2,1,0:T(8,128)(2,1)} %copy-done.9, bf16[128,64,512]{2,1,0:T(8,128)(2,1)} %rest_4_.1, ...), custom_call_target="tpu_custom_call" | custom-call | flops 17999998976 | bytes 1000 | tf_op jit(solution)/shard_map/finish/pallas_call | solution.py:367
  (10 shorter events, 0.2 us)
Async XLA Ops:
  6.5 12.1 %copy-start = (bf16[32,16384]{1,0:T(8,128)(2,1)S(1)}, bf16[32,16384]{1,0:T(8,128)(2,1)}, u32[]{:S(2)}) copy-start(bf16[32,16384]{1,0:T(8,128)(2,1)} %x_ref.3) | copy-start | bytes 3145732
  6.5 98.0 %all-gather.2.cloned.1.call-start = ((), (), s32[]{:S(2)}) async-start(), calls=%async_computation | async-start | bytes 4718592 | tf_op jit(solution)/shard_map/all_gather | solution.py:399
  11.6 7.1 %copy-start.1 = (s32[2,16384]{1,0:T(2,128)S(1)}, s32[2,16384]{1,0:T(2,128)}, u32[]{:S(2)}) copy-start(s32[2,16384]{1,0:T(2,128)} %param.11) | copy-start | bytes 393220
  11.6 14.5 %copy-start.2 = (bf16[16,32,128]{2,1,0:T(8,128)(2,1)S(1)}, bf16[16,32,128]{2,1,0:T(8,128)(2,1)}, u32[]{:S(2)}) copy-start(bf16[16,32,128]{2,1,0:T(8,128)(2,1)} %get-tuple-element.10) | copy-start | bytes 393220
  11.6 12.1 %collective-permute-start.5 = (bf16[16,32,128]{2,1,0:T(8,128)(2,1)}, bf16[16,32,128]{2,1,0:T(8,128)(2,1)S(1)}, u32[]{:S(2)}, u32[]{:S(2)}) collective-permute-start(bf16[16,32,128]{2,1,0:T(8,128)(2,1)} %get-tuple-element.10), channel_id=1, source_target_pairs={{0,1},{1,2},{2,3},{3,0},{4,5},{5,6},{6,7},{7,4},{8,9},{9,10},{10,1... | collective-permute-start | bytes 393224 | tf_op jit(solution)/shard_map/ppermute | solution.py:397
  14.7 11.5 %collective-permute-start.6 = (bf16[16,32,128]{2,1,0:T(8,128)(2,1)}, bf16[16,32,128]{2,1,0:T(8,128)(2,1)S(1)}, u32[]{:S(2)}, u32[]{:S(2)}) collective-permute-start(bf16[16,32,128]{2,1,0:T(8,128)(2,1)} %get-tuple-element.10), channel_id=1, source_target_pairs={{0,2},{1,3},{2,0},{3,1},{4,6},{5,7},{6,4},{7,5},{8,10},{9,11},{10,... | collective-permute-start | bytes 393224 | tf_op jit(solution)/shard_map/ppermute | solution.py:397
  17.3 8.9 %collective-permute-start.7 = (bf16[16,32,128]{2,1,0:T(8,128)(2,1)}, bf16[16,32,128]{2,1,0:T(8,128)(2,1)S(1)}, u32[]{:S(2)}, u32[]{:S(2)}) collective-permute-start(bf16[16,32,128]{2,1,0:T(8,128)(2,1)} %get-tuple-element.10), channel_id=1, source_target_pairs={{0,3},{1,0},{2,1},{3,2},{4,7},{5,4},{6,5},{7,6},{8,11},{9,8},{10,9... | collective-permute-start | bytes 393224 | tf_op jit(solution)/shard_map/ppermute | solution.py:397
  18.7 9.1 %copy-start.4 = (s32[128,9]{0,1:T(8,128)S(1)}, s32[128,9]{0,1:T(8,128)}, u32[]{:S(2)}) copy-start(s32[128,9]{0,1:T(8,128)} %param.12) | copy-start | bytes 13828
  18.8 10.7 %copy-start.3 = (s32[32,27]{1,0:T(8,128)S(1)}, s32[32,27]{1,0:T(8,128)}, u32[]{:S(2)}) copy-start(s32[32,27]{1,0:T(8,128)} %param.14) | copy-start | bytes 10372
  18.8 11.5 %copy-start.5 = (s32[128,8]{0,1:T(8,128)S(1)}, s32[128,8]{0,1:T(8,128)}, u32[]{:S(2)}) copy-start(s32[128,8]{0,1:T(8,128)} %param.13) | copy-start | bytes 12292
  18.9 29.3 %collective-permute-start = (bf16[32,17408]{1,0:T(8,128)(2,1)S(1)}, bf16[32,17408]{1,0:T(8,128)(2,1)}, u32[]{:S(2)}, u32[]{:S(2)}) collective-permute-start(bf16[32,17408]{1,0:T(8,128)(2,1)S(1)} %constant_dynamic-update-slice_fusion), channel_id=1, source_target_pairs={{0,1},{1,2},{2,3},{3,4},{4,5},{5,6},{6,7},{7,8},{8,9},{9,10},{10,1... | collective-permute-start | bytes 3342344 | tf_op jit(solution)/shard_map/ppermute | solution.py:435
  22.5 51.4 %collective-permute-start.1 = (bf16[32,17408]{1,0:T(8,128)(2,1)S(1)}, bf16[32,17408]{1,0:T(8,128)(2,1)}, u32[]{:S(2)}, u32[]{:S(2)}) collective-permute-start(bf16[32,17408]{1,0:T(8,128)(2,1)S(1)} %constant_dynamic-update-slice_fusion), channel_id=1, source_target_pairs={{1,0},{2,1},{3,2},{4,3},{5,4},{6,5},{7,6},{8,7},{9,8},{10,9},{11,1... | collective-permute-start | bytes 3342344 | tf_op jit(solution)/shard_map/ppermute | solution.py:436
  31.1 42.8 %copy-start.6 = (bf16[32,32,256]{2,1,0:T(8,128)(2,1)S(1)}, bf16[32,32,256]{2,1,0:T(8,128)(2,1)}, u32[]{:S(2)}) copy-start(bf16[32,32,256]{2,1,0:T(8,128)(2,1)} %get-tuple-element.9.rest_0_) | copy-start | bytes 1572868
  73.9 46.6 %collective-permute-start.2 = (bf16[32,32,256]{2,1,0:T(8,128)(2,1)S(1)}, bf16[32,32,256]{2,1,0:T(8,128)(2,1)S(1)}, u32[]{:S(2)}, u32[]{:S(2)}) collective-permute-start(bf16[32,32,256]{2,1,0:T(8,128)(2,1)S(1)} %copy-done.6), channel_id=1, source_target_pairs={{0,1},{1,2},{2,3},{3,0},{4,5},{5,6},{6,7},{7,4},{8,9},{9,10},{10,1... | collective-permute-start | bytes 1572872 | tf_op jit(solution)/shard_map/ppermute | solution.py:406
  77.3 43.3 %collective-permute-start.3 = (bf16[32,32,256]{2,1,0:T(8,128)(2,1)S(1)}, bf16[32,32,256]{2,1,0:T(8,128)(2,1)S(1)}, u32[]{:S(2)}, u32[]{:S(2)}) collective-permute-start(bf16[32,32,256]{2,1,0:T(8,128)(2,1)S(1)} %copy-done.6), channel_id=1, source_target_pairs={{0,2},{1,3},{2,0},{3,1},{4,6},{5,7},{6,4},{7,5},{8,10},{9,11},{10,... | collective-permute-start | bytes 1572872 | tf_op jit(solution)/shard_map/ppermute | solution.py:406
  77.3 43.3 %collective-permute-start.4 = (bf16[32,32,256]{2,1,0:T(8,128)(2,1)S(1)}, bf16[32,32,256]{2,1,0:T(8,128)(2,1)S(1)}, u32[]{:S(2)}, u32[]{:S(2)}) collective-permute-start(bf16[32,32,256]{2,1,0:T(8,128)(2,1)S(1)} %copy-done.6), channel_id=1, source_target_pairs={{0,3},{1,0},{2,1},{3,2},{4,7},{5,4},{6,5},{7,6},{8,11},{9,8},{10,9... | collective-permute-start | bytes 1572872 | tf_op jit(solution)/shard_map/ppermute | solution.py:406
  120.5 0.8 copy-start.7
  120.6 1.0 copy-start.8
  121.5 0.8 copy-start.9
Sparse Core Ops, SparseCore 0:
  27.2 66.9 all-gather.1
